TPU v7x, 128 devices: a whole 4x4x4 slice. The times are simulated.
128 devices in a mesh: frame: 4 (over y_hi, core), slab: 32 (over y_lo, x, z).
Axes of the slice: x: 4, y: 4 (y_hi: 2, y_lo: 2; y = y_hi * 2 + y_lo), z: 4, core: 2. Of those that a mesh axis runs over, the one named last changes fastest.
Arguments:
- template: float32 [256, 32, 256], P('slab'), may hold values from -6 to 6
- displacement: float32 [8, 256, 32, 256], P('frame', 'slab'), may hold values from -8 to 8
- coil_images: bfloat16 [8, 2, 24, 256, 32, 256], P('frame', None, None, 'slab'), may hold values from -6 to 6
- sensitivities: bfloat16 [2, 24, 256, 32, 256], P(None, None, 'slab'), may hold values from -0.875 to 0.875
Outputs:
- refreshed_template: float32 [256, 32, 256], P('slab')
- new_displacement: float32 [8, 256, 32, 256], P('frame', 'slab')
All inputs are finite; a program needn't handle non-finite values.
Results may differ from a plain program's by a relative error of at most 0.0003.
Values sent between devices are 32-bit elements; how exact they have to be, the bound alone decides.
A program may use at most 128 MiB of HBM per device.

v0:
```python
import jax
import jax.numpy as jnp
from jax import lax
from jax.sharding import PartitionSpec as P

BOUND = 8
RADIUS = 4


def extended_2(cells, sides, width):
    for axis, dim in sides:
        count = lax.axis_size(axis)
        ends = count - 1
        head = lax.slice_in_dim(cells, 0, width, axis=dim)
        tail = lax.slice_in_dim(cells, cells.shape[dim] - width, cells.shape[dim], axis=dim)
        cells = jnp.concatenate(
            [
                lax.ppermute(tail, axis, [(i, (i + 1) % count) for i in range(ends)]),
                cells,
                lax.ppermute(head, axis, [((i + 1) % count, i) for i in range(ends)]),
            ],
            axis=dim,
        )
    return cells


def tent_weight(values):
    return jnp.maximum(0.0, 1.0 - jnp.abs(values))


def warp_planes(extended, displace, extent):
    planes = displace.shape[-3]
    summed = jnp.zeros(displace.shape, jnp.float32)
    for offset in range(-extent, extent + 1):
        source = extended[..., extent + offset : extent + offset + planes, :, :]
        summed = summed + tent_weight(displace - offset) * source
    return summed


def adjoint_planes(displace_ext, residual_ext, extent):
    planes = displace_ext.shape[-3] - 2 * extent
    summed = jnp.zeros(displace_ext.shape[:-3] + (planes,) + displace_ext.shape[-2:], jnp.float32)
    for offset in range(-extent, extent + 1):
        lower = extent - offset
        moved_from = displace_ext[..., lower : lower + planes, :, :]
        values = residual_ext[..., lower : lower + planes, :, :]
        summed = summed + tent_weight(moved_from - offset) * values
    return summed


def gauss_weights(radius):
    offsets_list = jnp.arange(-radius, radius + 1).astype(jnp.float32)
    spread = radius * 0.5
    unscaled = jnp.exp(-offsets_list * offsets_list / (2.0 * spread * spread))
    return unscaled / jnp.sum(unscaled)


def gauss_table(length, radius):
    indices = jnp.arange(length)
    apart = indices[:, None] - indices[None, :]
    distance = apart.astype(jnp.float32)
    spread = radius * 0.5
    offsets_list = jnp.arange(-radius, radius + 1).astype(jnp.float32)
    normalizer = jnp.sum(jnp.exp(-offsets_list * offsets_list / (2.0 * spread * spread)))
    unscaled = jnp.where(
        jnp.abs(apart) <= radius, jnp.exp(-distance * distance / (2.0 * spread * spread)), 0.0
    )
    return unscaled / normalizer


def smooth_field(extended, radius, planes):
    weights = gauss_weights(radius)
    summed = jnp.zeros(extended.shape[:-3] + (planes,) + extended.shape[-2:], jnp.float32)
    for offset in range(-radius, radius + 1):
        summed = (
            summed
            + weights[offset + radius]
            * extended[..., radius + offset : radius + offset + planes, :, :]
        )
    table_y = gauss_table(summed.shape[-1], radius)
    table_x = gauss_table(summed.shape[-2], radius)
    along_y = jnp.einsum("...xy,yw->...xw", summed, table_y, precision=lax.Precision.HIGHEST)
    return jnp.einsum("...xy,xv->...vy", along_y, table_x, precision=lax.Precision.HIGHEST)


def demons_step(displace, combined, template_ext, extent):
    planes = displace.shape[-3]
    warped_new = warp_planes(template_ext, displace, extent)
    mismatch = combined - warped_new
    interior = template_ext[extent : extent + planes]
    grad_z = (
        template_ext[extent + 1 : extent + 1 + planes]
        - template_ext[extent - 1 : extent - 1 + planes]
    ) * 0.5
    padded_x = jnp.pad(interior, ((0, 0), (1, 1), (0, 0)))
    grad_x = (padded_x[:, 2:, :] - padded_x[:, :-2, :]) * 0.5
    padded_y = jnp.pad(interior, ((0, 0), (0, 0), (1, 1)))
    grad_y = (padded_y[:, :, 2:] - padded_y[:, :, :-2]) * 0.5
    gradient_sq = grad_x * grad_x + grad_y * grad_y + grad_z * grad_z
    demons_force = mismatch * grad_z / (gradient_sq + mismatch * mismatch + 1.0)
    return displace + demons_force


def template_planes(volume):
    return extended_2(volume, (("slab", 0),), BOUND)


def per_device(template, displacement, coil_images, sensitivities):
    frames_all = displacement.shape[0] * lax.axis_size("frame")
    planes = displacement.shape[1]
    combined = jnp.einsum(
        "fpczxy,pczxy->fzxy", coil_images, sensitivities, preferred_element_type=jnp.float32
    )
    energy = jnp.einsum(
        "pczxy,pczxy->zxy", sensitivities, sensitivities, preferred_element_type=jnp.float32
    )
    warped = warp_planes(template_planes(template), displacement, BOUND)
    residual_back = combined - energy * warped
    stacked = jnp.stack([displacement, residual_back])
    extended = extended_2(stacked, (("slab", 2),), BOUND)
    adjoint = adjoint_planes(extended[0], extended[1], BOUND)
    summed_local = jnp.sum(adjoint, axis=0)
    summed = lax.psum(summed_local, "frame")
    refreshed_ext = template_planes(template + summed / frames_all)
    refreshed = refreshed_ext[BOUND : BOUND + planes]
    moved = demons_step(displacement, combined, refreshed_ext, BOUND)
    moved_ext = extended_2(moved, (("slab", 1),), RADIUS)
    smoothed = smooth_field(moved_ext, RADIUS, planes)
    return (refreshed, BOUND * jnp.tanh(smoothed / BOUND))


def solution(mesh):
    placed = (
        P("slab", None, None),
        P("frame", "slab", None, None),
        P("frame", None, None, "slab", None, None),
        P(None, None, "slab", None, None),
    )
    return jax.shard_map(
        per_device,
        mesh=mesh,
        in_specs=placed,
        out_specs=(P("slab", None, None), P("frame", "slab", None, None)),
        check_vma=False,
    )
```

profile of v0, /device:TPU:8, one launch (start us, length us, event | category | flops | bytes accessed | tf_op | source)
XLA Modules:
  0.0 172.7 jit_solution(16290382557970604666)
XLA Ops:
  7.2 0.0 all-reduce.4.cloned.1.call-start
  7.2 8.0 %collective-permute-start.1 = (f32[8,32,256]{2,1,0:T(8,128)}, f32[8,32,256]{2,1,0:T(8,128)}, u32[]{:S(2)}, u32[]{:S(2)}) collective-permute-start(f32[8,32,256]{2,1,0:T(8,128)} %param.4), channel_id=1, source_target_pairs={{1,0},{2,1},{3,2},{4,3},{5,4},{6,5},{7,6},{8,7},{9,8},{10,9},{11,1... | collective-permute-start | bytes 786440 | tf_op jit(solution)/shard_map/ppermute | solution.py:20
  15.2 1.9 %collective-permute-start = (f32[8,32,256]{2,1,0:T(8,128)}, f32[8,32,256]{2,1,0:T(8,128)}, u32[]{:S(2)}, u32[]{:S(2)}) collective-permute-start(f32[8,32,256]{2,1,0:T(8,128)} %param.4), channel_id=1, source_target_pairs={{0,1},{1,2},{2,3},{3,4},{4,5},{5,6},{6,7},{7,8},{8,9},{9,10},{10,1... | collective-permute-start | bytes 786440 | tf_op jit(solution)/shard_map/ppermute | solution.py:18
  17.2 0.0 slice-start
  17.2 4.5 %bitcast_convert_fusion = f32[8,32,256,24,2]{2,1,0,3,4:T(8,128)S(1)} fusion(bf16[2,24,8,32,256]{4,3,2,1,0:T(8,128)(2,1)} %param.7), kind=kLoop, calls=%fused_computation.2 | loop fusion | flops 3145728 | bytes 18874368
  21.7 0.0 slice-start.1
  21.8 7.8 %multiply_reduce_fusion = f32[8,32,256,2]{2,1,0,3:T(8,128)S(1)} fusion(f32[8,32,256,24,2]{2,1,0,3,4:T(8,128)S(1)} %bitcast_convert_fusion, bf16[2,2,24,8,32,256]{5,4,3,2,1,0:T(8,128)(2,1)} %param.6), kind=kLoop, calls=%fused_computation | loop fusion | flops 18743296 | bytes 25690112 | tf_op jit(solution)/shard_map/fpczxy,pczxy->fzxy/dot_general | solution.py:111
  29.6 0.0 copy-start.2
  29.6 1.5 multiply_reduce_fusion.1
  31.1 0.0 collective-permute-done
  31.1 1.0 constant_dynamic-update-slice_fusion.1
  32.1 0.0 copy-done.2
  32.2 0.0 collective-permute-done.1
  32.2 1.0 constant_dynamic-update-slice_fusion.2
  33.1 0.0 copy-start
  33.2 0.2 fusion.175
  33.4 0.2 fusion.174
  33.6 0.6 copy-done
  34.2 2.8 %fusion.103 = f32[1,2,8,32,256]{4,3,2,1,0:T(8,128)S(1)} fusion(f32[8,32,256,2]{2,1,0,3:T(8,128)S(1)} %multiply_reduce_fusion, f32[2,8,32,256]{3,2,1,0:T(8,128)S(1)} %copy-done, f32[8,32,256]{2,1,0:T(8,128)} %collective-permute-done.1, f32[8,32,256]{2,1,0:T(8,128)S(1)} %get-tuple-element.31, f32[8,32,256]{2,1,0:T(8,128)S(1)} %get-tuple-element.32, ...), kind=kLoop, calls=%fused_computation.177 | loop fusion | flops 13369344 | bytes 6291456 | tf_op jit(solution)/shard_map/stack | solution.py:119
  36.9 0.1 pad_maximum_fusion.1
  37.1 8.1 %collective-permute-start.3 = (f32[2,2,8,32,256]{4,3,2,1,0:T(8,128)S(1)}, f32[2,2,8,32,256]{4,3,2,1,0:T(8,128)S(1)}, u32[]{:S(2)}, u32[]{:S(2)}) collective-permute-start(f32[2,2,8,32,256]{4,3,2,1,0:T(8,128)S(1)} %pad_maximum_fusion.1), channel_id=1, source_target_pairs={{1,0},{2,1},{3,2},{4,3},{5,4},{6,5},{7,6},{8,7},{9,8},{10,9},{11,1... | collective-permute-start | bytes 3145736 | tf_op jit(solution)/shard_map/ppermute | solution.py:20
  45.2 1.9 %collective-permute-start.2 = (f32[2,2,8,32,256]{4,3,2,1,0:T(8,128)S(1)}, f32[2,2,8,32,256]{4,3,2,1,0:T(8,128)S(1)}, u32[]{:S(2)}, u32[]{:S(2)}) collective-permute-start(f32[2,2,8,32,256]{4,3,2,1,0:T(8,128)S(1)} %pad_maximum_fusion.1), channel_id=1, source_target_pairs={{0,1},{1,2},{2,3},{3,4},{4,5},{5,6},{6,7},{7,8},{8,9},{9,10},{10,1... | collective-permute-start | bytes 3145736 | tf_op jit(solution)/shard_map/ppermute | solution.py:18
  47.1 19.9 %collective-permute-done.3 = f32[2,2,8,32,256]{4,3,2,1,0:T(8,128)S(1)} collective-permute-done((f32[2,2,8,32,256]{4,3,2,1,0:T(8,128)S(1)}, f32[2,2,8,32,256]{4,3,2,1,0:T(8,128)S(1)}, u32[]{:S(2)}, u32[]{:S(2)}) %collective-permute-start.3) | collective-permute-done | bytes 1048608 | tf_op jit(solution)/shard_map/ppermute | solution.py:20
  67.0 8.3 %collective-permute-done.2 = f32[2,2,8,32,256]{4,3,2,1,0:T(8,128)S(1)} collective-permute-done((f32[2,2,8,32,256]{4,3,2,1,0:T(8,128)S(1)}, f32[2,2,8,32,256]{4,3,2,1,0:T(8,128)S(1)}, u32[]{:S(2)}, u32[]{:S(2)}) %collective-permute-start.2) | collective-permute-done | bytes 1048608 | tf_op jit(solution)/shard_map/ppermute | solution.py:18
  75.4 0.4 pad_maximum_fusion
  75.8 0.4 slice_bitcast_fusion.1
  76.2 3.0 %fusion.37 = f32[8,32,256]{2,1,0:T(8,128)} fusion(f32[2,24,32,256]{3,2,1,0:T(8,128)S(1)} %get-tuple-element.6, f32[2,24,32,256]{3,2,1,0:T(8,128)S(1)} %get-tuple-element.5), kind=kLoop, calls=%fused_computation.76 | loop fusion | flops 13172736 | bytes 18087936 | tf_op jit(solution)/shard_map/reduce_sum | solution.py:122
  79.2 0.0 all-reduce.4.cloned.1.call-update
  79.2 36.2 %all-reduce.4.cloned.1.call-done = f32[8,32,256]{2,1,0:T(8,128)} async-done(((f32[8,32,256]{2,1,0:T(8,128)}), f32[8,32,256]{2,1,0:T(8,128)}) %all-reduce.4.cloned.1.call-update) | async-done | bytes 262160 | tf_op jit(solution)/shard_map/psum | solution.py:123
  115.5 1.0 multiply_add_fusion
  116.4 0.0 copy-start.1
  116.5 7.9 %collective-permute-start.5 = (f32[8,32,256]{2,1,0:T(8,128)S(1)}, f32[8,32,256]{2,1,0:T(8,128)S(1)}, u32[]{:S(2)}, u32[]{:S(2)}) collective-permute-start(f32[8,32,256]{2,1,0:T(8,128)S(1)} %multiply_add_fusion), channel_id=1, source_target_pairs={{1,0},{2,1},{3,2},{4,3},{5,4},{6,5},{7,6},{8,7},{9,8},{10,9},{11,1... | collective-permute-start | bytes 786440 | tf_op jit(solution)/shard_map/ppermute | solution.py:20
  124.3 1.9 %collective-permute-start.4 = (f32[8,32,256]{2,1,0:T(8,128)S(1)}, f32[8,32,256]{2,1,0:T(8,128)S(1)}, u32[]{:S(2)}, u32[]{:S(2)}) collective-permute-start(f32[8,32,256]{2,1,0:T(8,128)S(1)} %multiply_add_fusion), channel_id=1, source_target_pairs={{0,1},{1,2},{2,3},{3,4},{4,5},{5,6},{6,7},{7,8},{8,9},{9,10},{10,1... | collective-permute-start | bytes 786440 | tf_op jit(solution)/shard_map/ppermute | solution.py:18
  126.2 4.1 %collective-permute-done.5 = f32[8,32,256]{2,1,0:T(8,128)S(1)} collective-permute-done((f32[8,32,256]{2,1,0:T(8,128)S(1)}, f32[8,32,256]{2,1,0:T(8,128)S(1)}, u32[]{:S(2)}, u32[]{:S(2)}) %collective-permute-start.5) | collective-permute-done | bytes 262176 | tf_op jit(solution)/shard_map/ppermute | solution.py:20
  130.4 8.3 %collective-permute-done.4 = f32[8,32,256]{2,1,0:T(8,128)S(1)} collective-permute-done((f32[8,32,256]{2,1,0:T(8,128)S(1)}, f32[8,32,256]{2,1,0:T(8,128)S(1)}, u32[]{:S(2)}, u32[]{:S(2)}) %collective-permute-start.4) | collective-permute-done | bytes 262176 | tf_op jit(solution)/shard_map/ppermute | solution.py:18
  138.7 0.2 fusion.126
  138.9 0.4 fusion.121
  139.3 0.0 copy-done.1
  139.3 1.9 %divide_add_fusion = f32[2,8,32,256]{3,2,1,0:T(8,128)S(1)} fusion(f32[2,8,32,256]{3,2,1,0:T(8,128)S(1)} %copy-done, f32[8,32,256,2]{2,1,0,3:T(8,128)S(1)} %multiply_reduce_fusion, f32[8,32,256]{2,1,0:T(8,128)S(1)} %get-tuple-element.38, f32[8,32,256]{2,1,0:T(8,128)S(1)} %get-tuple-element.14, f32[8,32,256]{2,1,0:T(8,128)S(1)} %collective-permute-done.5, ...), kind=kLoop, calls=%fused_computation.179 | loop fusion | flops 14024704 | bytes 6553600 | tf_op jit(solution)/shard_map/add | solution.py:101
  141.3 1.9 %collective-permute-start.7 = (f32[2,4,32,256]{3,2,1,0:T(8,128)S(1)}, f32[2,4,32,256]{3,2,1,0:T(8,128)S(1)}, u32[]{:S(2)}, u32[]{:S(2)}) collective-permute-start(f32[2,4,32,256]{3,2,1,0:T(8,128)S(1)} %get-tuple-element.8), channel_id=1, source_target_pairs={{1,0},{2,1},{3,2},{4,3},{5,4},{6,5},{7,6},{8,7},{9,8},{10,9},{11,1... | collective-permute-start | bytes 786440 | tf_op jit(solution)/shard_map/ppermute | solution.py:20
  143.2 3.9 %collective-permute-start.6 = (f32[2,4,32,256]{3,2,1,0:T(8,128)S(1)}, f32[2,4,32,256]{3,2,1,0:T(8,128)S(1)}, u32[]{:S(2)}, u32[]{:S(2)}) collective-permute-start(f32[2,4,32,256]{3,2,1,0:T(8,128)S(1)} %get-tuple-element.7), channel_id=1, source_target_pairs={{0,1},{1,2},{2,3},{3,4},{4,5},{5,6},{6,7},{7,8},{8,9},{9,10},{10,1... | collective-permute-start | bytes 786440 | tf_op jit(solution)/shard_map/ppermute | solution.py:18
  147.1 0.7 fusion.164
  147.8 0.6 broadcast_divide_fusion
  148.4 0.7 fusion.176
  149.1 1.5 collective-permute-done.7
  150.6 6.1 %collective-permute-done.6 = f32[2,4,32,256]{3,2,1,0:T(8,128)S(1)} collective-permute-done((f32[2,4,32,256]{3,2,1,0:T(8,128)S(1)}, f32[2,4,32,256]{3,2,1,0:T(8,128)S(1)}, u32[]{:S(2)}, u32[]{:S(2)}) %collective-permute-start.6) | collective-permute-done | bytes 262176 | tf_op jit(solution)/shard_map/ppermute | solution.py:18
  156.7 7.2 %fusion.7 = f32[2,8,32,256]{3,2,1,0:T(8,128)S(1)} fusion(f32[2,8,32,256]{3,2,1,0:T(8,128)S(1)} %divide_add_fusion, f32[2,4,32,256]{3,2,1,0:T(8,128)S(1)} %collective-permute-done.7, f32[2,4,32,256]{3,2,1,0:T(8,128)S(1)} %collective-permute-done.6, f32[]{:T(128)} %bitcast.19, f32[]{:T(128)} %bitcast.18, f32[]{:T(128)} %bitcast.17, f32[]{:T(128)} %bitcast.16, ...), kind=kOutput, calls=%fused_computation.51 | convolution fusion | flops 406519808 | bytes 1572904 | tf_op jit(solution)/shard_map/...xy,yw->...xw/dot_general | solution.py:82
  163.9 2.0 %fusion.2 = f32[2,8,32,256]{3,2,1,0:T(8,128)} fusion(f32[2,8,32,256]{3,2,1,0:T(8,128)S(1)} %fusion.7, f32[]{:T(128)} %fusion.164), kind=kOutput, calls=%fused_computation.9 | convolution fusion | flops 50603008 | bytes 1048580 | tf_op jit(solution)/shard_map/...xy,xv->...vy/dot_general | solution.py:83
  (5 shorter events, 0.1 us)
Async XLA Ops:
  7.2 108.3 %all-reduce.4.cloned.1.call-start = ((), (), s32[]{:S(2)}) async-start(), calls=%async_computation | async-start | bytes 524288 | tf_op jit(solution)/shard_map/psum | solution.py:123
  7.2 25.0 %collective-permute-start.1 = (f32[8,32,256]{2,1,0:T(8,128)}, f32[8,32,256]{2,1,0:T(8,128)}, u32[]{:S(2)}, u32[]{:S(2)}) collective-permute-start(f32[8,32,256]{2,1,0:T(8,128)} %param.4), channel_id=1, source_target_pairs={{1,0},{2,1},{3,2},{4,3},{5,4},{6,5},{7,6},{8,7},{9,8},{10,9},{11,1... | collective-permute-start | bytes 786440 | tf_op jit(solution)/shard_map/ppermute | solution.py:20
  15.2 15.9 %collective-permute-start = (f32[8,32,256]{2,1,0:T(8,128)}, f32[8,32,256]{2,1,0:T(8,128)}, u32[]{:S(2)}, u32[]{:S(2)}) collective-permute-start(f32[8,32,256]{2,1,0:T(8,128)} %param.4), channel_id=1, source_target_pairs={{0,1},{1,2},{2,3},{3,4},{4,5},{5,6},{6,7},{7,8},{8,9},{9,10},{10,1... | collective-permute-start | bytes 786440 | tf_op jit(solution)/shard_map/ppermute | solution.py:18
  17.2 12.4 %slice-start = ((s8[6291456]{0:T(1024)(128)(4,1)}), s8[4194304]{0:T(1024)(128)(4,1)S(1)}, s32[]{:S(2)}) async-start(s8[6291456]{0:T(1024)(128)(4,1)} %bitcast.44), calls=%async_computation.1 | async-start | bytes 8388608
  21.7 7.8 %slice-start.1 = ((s8[6291456]{0:T(1024)(128)(4,1)}), s8[2097152]{0:T(1024)(128)(4,1)S(1)}, s32[]{:S(2)}) async-start(s8[6291456]{0:T(1024)(128)(4,1)} %bitcast.44), calls=%async_computation.2 | async-start | bytes 4194304
  29.6 2.5 %copy-start.2 = (f32[8,32,256]{2,1,0:T(8,128)S(1)}, f32[8,32,256]{2,1,0:T(8,128)}, u32[]{:S(2)}) copy-start(f32[8,32,256]{2,1,0:T(8,128)} %param.4) | copy-start | bytes 786436
  33.1 1.0 copy-start
  37.1 30.0 %collective-permute-start.3 = (f32[2,2,8,32,256]{4,3,2,1,0:T(8,128)S(1)}, f32[2,2,8,32,256]{4,3,2,1,0:T(8,128)S(1)}, u32[]{:S(2)}, u32[]{:S(2)}) collective-permute-start(f32[2,2,8,32,256]{4,3,2,1,0:T(8,128)S(1)} %pad_maximum_fusion.1), channel_id=1, source_target_pairs={{1,0},{2,1},{3,2},{4,3},{5,4},{6,5},{7,6},{8,7},{9,8},{10,9},{11,1... | collective-permute-start | bytes 3145736 | tf_op jit(solution)/shard_map/ppermute | solution.py:20
  45.2 30.2 %collective-permute-start.2 = (f32[2,2,8,32,256]{4,3,2,1,0:T(8,128)S(1)}, f32[2,2,8,32,256]{4,3,2,1,0:T(8,128)S(1)}, u32[]{:S(2)}, u32[]{:S(2)}) collective-permute-start(f32[2,2,8,32,256]{4,3,2,1,0:T(8,128)S(1)} %pad_maximum_fusion.1), channel_id=1, source_target_pairs={{0,1},{1,2},{2,3},{3,4},{4,5},{5,6},{6,7},{7,8},{8,9},{9,10},{10,1... | collective-permute-start | bytes 3145736 | tf_op jit(solution)/shard_map/ppermute | solution.py:18
  116.4 22.8 %copy-start.1 = (f32[8,32,256]{2,1,0:T(8,128)}, f32[8,32,256]{2,1,0:T(8,128)S(1)}, u32[]{:S(2)}) copy-start(f32[8,32,256]{2,1,0:T(8,128)S(1)} %multiply_add_fusion) | copy-start | bytes 786436
  116.5 13.9 %collective-permute-start.5 = (f32[8,32,256]{2,1,0:T(8,128)S(1)}, f32[8,32,256]{2,1,0:T(8,128)S(1)}, u32[]{:S(2)}, u32[]{:S(2)}) collective-permute-start(f32[8,32,256]{2,1,0:T(8,128)S(1)} %multiply_add_fusion), channel_id=1, source_target_pairs={{1,0},{2,1},{3,2},{4,3},{5,4},{6,5},{7,6},{8,7},{9,8},{10,9},{11,1... | collective-permute-start | bytes 786440 | tf_op jit(solution)/shard_map/ppermute | solution.py:20
  124.3 14.4 %collective-permute-start.4 = (f32[8,32,256]{2,1,0:T(8,128)S(1)}, f32[8,32,256]{2,1,0:T(8,128)S(1)}, u32[]{:S(2)}, u32[]{:S(2)}) collective-permute-start(f32[8,32,256]{2,1,0:T(8,128)S(1)} %multiply_add_fusion), channel_id=1, source_target_pairs={{0,1},{1,2},{2,3},{3,4},{4,5},{5,6},{6,7},{7,8},{8,9},{9,10},{10,1... | collective-permute-start | bytes 786440 | tf_op jit(solution)/shard_map/ppermute | solution.py:18
  141.3 9.3 %collective-permute-start.7 = (f32[2,4,32,256]{3,2,1,0:T(8,128)S(1)}, f32[2,4,32,256]{3,2,1,0:T(8,128)S(1)}, u32[]{:S(2)}, u32[]{:S(2)}) collective-permute-start(f32[2,4,32,256]{3,2,1,0:T(8,128)S(1)} %get-tuple-element.8), channel_id=1, source_target_pairs={{1,0},{2,1},{3,2},{4,3},{5,4},{6,5},{7,6},{8,7},{9,8},{10,9},{11,1... | collective-permute-start | bytes 786440 | tf_op jit(solution)/shard_map/ppermute | solution.py:20
  143.2 13.5 %collective-permute-start.6 = (f32[2,4,32,256]{3,2,1,0:T(8,128)S(1)}, f32[2,4,32,256]{3,2,1,0:T(8,128)S(1)}, u32[]{:S(2)}, u32[]{:S(2)}) collective-permute-start(f32[2,4,32,256]{3,2,1,0:T(8,128)S(1)} %get-tuple-element.7), channel_id=1, source_target_pairs={{0,1},{1,2},{2,3},{3,4},{4,5},{5,6},{6,7},{7,8},{8,9},{9,10},{10,1... | collective-permute-start | bytes 786440 | tf_op jit(solution)/shard_map/ppermute | solution.py:18
Sparse Core Ops, SparseCore 0:
  79.4 36.0 all-reduce.3
where the time goes:
time: 173 us
  waiting for transfers between devices  84.5 us (49%)
  starting transfers between devices  35.7 us (21%)
  other arithmetic  24.9 us (14%)
  between operations  14.3 us (8%)
  matrix products  9.17 us (5%)
  local copies, waits for them, and re-layouts  4.17 us (2%)
    psum x1, waiting for transfers between devices, per_device(): summed = lax.psum(summed_local, 'frame')  36.2 us
    ppermute x4, starting transfers between devices, extended_2(): lax.ppermute(head, axis, [((i + 1) % count, i) for i in range(ends)])  25.9 us
    ppermute x4, waiting for transfers between devices, extended_2(): lax.ppermute(head, axis, [((i + 1) % count, i) for i in range(ends)])  25.5 us
    ppermute x4, waiting for transfers between devices, extended_2(): lax.ppermute(tail, axis, [(i, (i + 1) % count) for i in range(ends)])  22.8 us
    ppermute x4, starting transfers between devices, extended_2(): lax.ppermute(tail, axis, [(i, (i + 1) % count) for i in range(ends)])  9.69 us
    dot_general x1, other arithmetic, per_device(): jnp.einsum('fpczxy,pczxy->fzxy', coil_images, sensitivities, preferred_el...  7.81 us
    dot_general x1, matrix products, smooth_field(): jnp.einsum('...xy,yw->...xw', summed, table_y, precision=lax.Precision.HI...  7.16 us
    unnamed x2, other arithmetic  4.54 us
  transfers between devices with their start and end apart: 9, of which 7 were waited for; matrix products, arithmetic and copies ran while one was open for 10% of the time, Pallas kernels for 0%

commit v1 on v0

v1 whole, which is shorter than its diff:
```python
import functools

import jax
import jax.numpy as jnp
import numpy as np
from jax import lax
from jax.experimental import pallas as pl
from jax.experimental.pallas import tpu as pltpu
from jax.sharding import PartitionSpec as P

BOUND = 8
RADIUS = 4
ROWS = 8
LANES = 128
CHUNK = 16
GROUPS = 4
MESH = pl.DeviceIdType.MESH
F32 = jnp.float32
BF16 = jnp.bfloat16


def gauss_weights():
    j = np.arange(-RADIUS, RADIUS + 1, dtype=np.float64)
    spread = RADIUS * 0.5
    w = np.exp(-j * j / (2.0 * spread * spread))
    return w / w.sum()


def gauss_table(length):
    w = gauss_weights()
    table = np.zeros((length, length), np.float64)
    for j in range(-RADIUS, RADIUS + 1):
        table += w[j + RADIUS] * np.eye(length, k=j)
    return table


def split_table(table):
    hi = table.astype(np.float32).astype(BF16)
    lo = (table - hi.astype(np.float64)).astype(np.float32).astype(BF16)
    return hi, lo


def locate(d):
    m3 = d >= 0.0
    r = jnp.where(m3, d, d + 8.0)
    m2 = r >= 4.0
    r = jnp.where(m2, r - 4.0, r)
    m1 = r >= 2.0
    r = jnp.where(m1, r - 2.0, r)
    m0 = r >= 1.0
    t = jnp.where(m0, r - 1.0, r)
    return m3, m2, m1, m0, t


def gather_line(place, plane):
    m3, m2, m1, m0, t = place
    a = [plane(j) for j in range(17)]
    b = [jnp.where(m3, a[j + 8], a[j]) for j in range(9)]
    c = [jnp.where(m2, b[j + 4], b[j]) for j in range(5)]
    e = [jnp.where(m1, c[j + 2], c[j]) for j in range(3)]
    lo = jnp.where(m0, e[1], e[0])
    hi = jnp.where(m0, e[2], e[1])
    return lo + t * (hi - lo)


def scatter_line(place, value):
    m3, m2, m1, m0, t = place
    hi = t * value
    lo = value - hi
    zero = jnp.zeros_like(value)
    e = [jnp.where(m0, zero, lo), jnp.where(m0, lo, hi), jnp.where(m0, hi, zero)]

    def spread(src, mask, step):
        n = len(src)
        out = []
        for j in range(n + step):
            low = src[j] if j < n else zero
            high = src[j - step] if j >= step else zero
            out.append(jnp.where(mask, high, low))
        return out

    return spread(spread(spread(e, m1, 2), m2, 4), m3, 8)


def kernel(cfg, tmpl, disp, coil, sens, ty_hi_h, ty_lo_h, kx_hi_h, kx_lo_h, out_t, out_d,
           tx, rx, dv, cb, sb, comb, ener, adj, radj, rlo, rhi, csum, rc, mv, gz, gs,
           shi, slo, obuf, ty_hi, ty_lo, kx_hi, kx_lo, lsem, ssem, rsem):
    n_slab, frames_all, coils = cfg
    nf, planes = dv.shape[0], dv.shape[1]
    wide = dv.shape[2]
    ny = dv.shape[3]
    n_rb = wide // ROWS
    n_chunk = wide // CHUNK
    per = planes // GROUPS
    f = lax.axis_index("frame")
    s = lax.axis_index("slab")
    h = lax.rem(f, 2)
    mate = f + 1 - 2 * h
    across = lax.rem(f + 2, 4)
    above = lax.rem(s + 1, n_slab)
    below = lax.rem(s + n_slab - 1, n_slab)
    has_above = s < n_slab - 1
    has_below = s > 0
    to_mate, to_across = (mate, s), (across, s)
    to_above, to_below = (f, above), (f, below)

    counter = [0]

    def local(src, dst):
        copy = pltpu.make_async_copy(src, dst, lsem.at[counter[0]])
        counter[0] += 1
        copy.start()
        return copy

    load_t = [local(tmpl.at[:, pl.ds(ROWS * b, ROWS), :], tx.at[b, pl.ds(BOUND, planes)]) for b in range(n_rb)]
    load_d = local(disp, dv)
    load_c = {}
    for c in range(n_chunk):
        for g in range(GROUPS):
            zs, xs = pl.ds(per * g, per), pl.ds(CHUNK * c, CHUNK)
            load_c[c, g] = (
                local(sens.at[:, :, zs, xs, :], sb.at[c, g]),
                local(coil.at[:, :, :, zs, xs, :], cb.at[c, g]),
            )
    load_k = [local(a, b) for a, b in ((ty_hi_h, ty_hi), (ty_lo_h, ty_lo), (kx_hi_h, kx_hi), (kx_lo_h, kx_lo))]

    barrier = pltpu.get_barrier_semaphore()
    for dev in (to_mate, to_across, to_above, to_below):
        pl.semaphore_signal(barrier, inc=1, device_id=dev, device_id_type=MESH)
    pl.semaphore_wait(barrier, 4)

    rcount = [0]
    pending = []

    class Remote:
        def __init__(self, src, dst, dev, send_if=None, recv_if=None):
            n = rcount[0]
            rcount[0] += 1
            self.copy = pltpu.make_async_remote_copy(
                src_ref=src, dst_ref=dst, send_sem=ssem.at[n], recv_sem=rsem.at[n],
                device_id=dev, device_id_type=MESH)
            self.send_if, self.recv_if = send_if, recv_if
            if send_if is None:
                self.copy.start()
            else:
                pl.when(send_if)(lambda: self.copy.start())
            pending.append(self)

        def recv(self):
            if self.recv_if is None:
                self.copy.wait_recv()
            else:
                pl.when(self.recv_if)(lambda: self.copy.wait_recv())

        def sent(self):
            if self.send_if is None:
                self.copy.wait_send()
            else:
                pl.when(self.send_if)(lambda: self.copy.wait_send())

    def up(src, dst):
        return Remote(src, dst, to_above, has_above, has_below)

    def down(src, dst):
        return Remote(src, dst, to_below, has_below, has_above)

    own = pl.ds(BOUND, planes)
    low = pl.ds(0, BOUND)
    high = pl.ds(BOUND + planes, BOUND)
    wire = {}

    def zero_edges(clear_low, clear_high):
        @pl.when(s == 0)
        def _():
            for ref, *index in clear_low:
                ref[tuple(index)] = jnp.zeros_like(ref[tuple(index)])

        @pl.when(s == n_slab - 1)
        def _():
            for ref, *index in clear_high:
                ref[tuple(index)] = jnp.zeros_like(ref[tuple(index)])

    def template_out(c):
        rb = 2 * c + h
        wire["tu", c] = up(tx.at[rb, own], tx.at[rb, low])
        wire["td", c] = down(tx.at[rb, own], tx.at[rb, high])

    def template_pass(c):
        rb = 2 * c + h
        wire["tu", c].recv()
        wire["td", c].recv()
        wire["tfl", c] = Remote(tx.at[rb, low], tx.at[rb, low], to_mate, has_below, has_below)
        wire["tfh", c] = Remote(tx.at[rb, high], tx.at[rb, high], to_mate, has_above, has_above)

    def template_in(c):
        wire["tfl", c].recv()
        wire["tfh", c].recv()

    def combine(c, g):
        for copy in load_c[c, g]:
            copy.wait()

        def step(zz, _):
            acc = None
            for p in range(2):
                for k in range(coils):
                    w = sb[c, g, p, k, zz].astype(F32)
                    vals = [cb[c, g, i, p, k, zz].astype(F32) * w for i in range(nf)] + [w * w]
                    acc = vals if acc is None else [x + v for x, v in zip(acc, vals)]
            z = per * g + zz
            xs = pl.ds(CHUNK * c, CHUNK)
            for i in range(nf):
                comb[i, z, xs, :] = acc[i]
            ener[z, xs, :] = acc[nf]
            return 0

        lax.fori_loop(0, per, step, 0)

    def tile(i):
        rbl = lax.div(i, ny // LANES)
        lh = lax.rem(i, ny // LANES)
        return rbl, pl.ds(pl.multiple_of(lh * LANES, LANES), LANES)

    def adjoint(c):
        def step(i, _):
            rbl, lanes = tile(i)
            rb = 2 * c + rbl
            rows = pl.ds(pl.multiple_of(rb * ROWS, ROWS), ROWS)
            sums = [None] * (planes + 2 * BOUND)
            for z in range(planes):
                en = ener[z, rows, lanes]
                for i_f in range(nf):
                    place = locate(dv[i_f, z, rows, lanes])
                    warped = gather_line(place, lambda j: tx[rb, z + j, :, lanes])
                    value = comb[i_f, z, rows, lanes] - en * warped
                    for j, term in enumerate(scatter_line(place, value)):
                        sums[z + j] = term if sums[z + j] is None else sums[z + j] + term
            for q, total in enumerate(sums):
                adj[rb, q, :, lanes] = total
            return 0

        lax.fori_loop(0, 2 * (ny // LANES), step, 0)

    def adj_mate(c):
        other = 2 * c + 1 - h
        wire["am", c] = Remote(adj.at[other], radj.at[c], to_mate)

    def adj_slab(c):
        rb = 2 * c + h
        wire["am", c].recv()
        for part in (low, high):
            adj[rb, part] = adj[rb, part] + radj[c, part]
        wire["au", c] = up(adj.at[rb, high], rlo.at[c])
        wire["ad", c] = down(adj.at[rb, low], rhi.at[c])
        csum[c] = adj[rb, own] + radj[c, own]

    def adj_across(c):
        wire["au", c].recv()
        wire["ad", c].recv()
        csum[c] = csum[c] + (rlo[c] + rhi[c])
        wire["ac", c] = Remote(csum.at[c], rc.at[c], to_across)

    def refresh(c):
        rb = 2 * c + h
        wire["ac", c].recv()
        rx[rb, own] = tx[rb, own] + (csum[c] + rc[c]) * (1.0 / frames_all)
        wire["rm", c] = Remote(rx.at[rb, own], rx.at[rb, own], to_mate)
        wire["ru", c] = up(rx.at[rb, own], rx.at[rb, low])
        wire["rd", c] = down(rx.at[rb, own], rx.at[rb, high])

    def refresh_pass(c):
        rb = 2 * c + h
        wire["ru", c].recv()
        wire["rd", c].recv()
        wire["rfl", c] = Remote(rx.at[rb, low], rx.at[rb, low], to_mate, has_below, has_below)
        wire["rfh", c] = Remote(rx.at[rb, high], rx.at[rb, high], to_mate, has_above, has_above)

    def refresh_in(c):
        wire["rm", c].recv()
        wire["rfl", c].recv()
        wire["rfh", c].recv()

    saves = []

    def save_template(b):
        saves.append(local(rx.at[b, own], out_t.at[:, pl.ds(ROWS * b, ROWS), :]))

    def gradients(b):
        first = lax.broadcasted_iota(jnp.int32, (ROWS, ny), 0) == 0
        last = lax.broadcasted_iota(jnp.int32, (ROWS, ny), 0) == ROWS - 1
        left = lax.broadcasted_iota(jnp.int32, (ROWS, ny), 1) == 0
        right = lax.broadcasted_iota(jnp.int32, (ROWS, ny), 1) == ny - 1

        def step(z, _):
            here = rx[b, BOUND + z]
            down_edge = pltpu.roll(rx[b - 1, BOUND + z], 1, 0) if b > 0 else jnp.zeros_like(here)
            up_edge = pltpu.roll(rx[b + 1, BOUND + z], ROWS - 1, 0) if b < n_rb - 1 else jnp.zeros_like(here)
            prev_x = jnp.where(first, down_edge, pltpu.roll(here, 1, 0))
            next_x = jnp.where(last, up_edge, pltpu.roll(here, ROWS - 1, 0))
            prev_y = jnp.where(left, 0.0, pltpu.roll(here, 1, 1))
            next_y = jnp.where(right, 0.0, pltpu.roll(here, ny - 1, 1))
            gx = (next_x - prev_x) * 0.5
            gy = (next_y - prev_y) * 0.5
            g_z = (rx[b, BOUND + z + 1] - rx[b, BOUND + z - 1]) * 0.5
            gz[b, z] = g_z
            gs[b, z] = gx * gx + gy * gy + g_z * g_z
            return 0

        lax.fori_loop(0, planes, step, 0)

    def force(b):
        rows = pl.ds(b * ROWS, ROWS)

        def step(lh, _):
            lanes = pl.ds(pl.multiple_of(lh * LANES, LANES), LANES)
            for z in range(planes):
                for i_f in range(nf):
                    d = dv[i_f, z, rows, lanes]
                    warped = gather_line(locate(d), lambda j: rx[b, z + j, :, lanes])
                    miss = comb[i_f, z, rows, lanes] - warped
                    push = miss * gz[b, z, :, lanes] / (gs[b, z, :, lanes] + miss * miss + 1.0)
                    mv[i_f, RADIUS + z, rows, lanes] = d + push
            return 0

        lax.fori_loop(0, ny // LANES, step, 0)

    def moved_out(b):
        rows = pl.ds(b * ROWS, ROWS)
        head, tail = pl.ds(RADIUS, RADIUS), pl.ds(planes, RADIUS)
        wire["mu", b] = up(mv.at[:, tail, rows, :], mv.at[:, pl.ds(0, RADIUS), rows, :])
        wire["md", b] = down(mv.at[:, head, rows, :], mv.at[:, pl.ds(planes + RADIUS, RADIUS), rows, :])

    weights = [float(w) for w in gauss_weights()]

    def halves(value):
        hi = value.astype(BF16)
        return hi, (value - hi.astype(F32)).astype(BF16)

    def dot3(a_hi, a_lo, b_hi, b_lo):
        dot = functools.partial(jnp.dot, preferred_element_type=F32)
        return dot(a_hi, b_hi) + (dot(a_lo, b_hi) + dot(a_hi, b_lo))

    def smooth(i_f):
        def step(z, _):
            total = None
            for j in range(2 * RADIUS + 1):
                term = weights[j] * mv[i_f, z + j]
                total = term if total is None else total + term
            hi, lo = halves(total)
            at = pl.ds(pl.multiple_of(z * wide, wide), wide)
            shi[at, :] = hi
            slo[at, :] = lo
            return 0

        lax.fori_loop(0, planes, step, 0)
        along_y = dot3(shi[...], slo[...], ty_hi[...], ty_lo[...])
        y_hi, y_lo = halves(along_y)
        done = dot3(kx_hi[...], kx_lo[...], y_hi, y_lo)
        obuf[i_f] = (BOUND * jnp.tanh(done * (1.0 / BOUND))).reshape(planes, wide, ny)
        saves.append(local(obuf.at[i_f], out_d.at[i_f]))

    for copy in load_t:
        copy.wait()
    for c in range(n_chunk):
        template_out(c)
    zero_edges([(tx, slice(None), slice(0, BOUND)), (rx, slice(None), slice(0, BOUND)), (rlo,),
                (mv, slice(None), slice(0, RADIUS))],
               [(tx, slice(None), slice(BOUND + planes, None)), (rx, slice(None), slice(BOUND + planes, None)),
                (rhi,), (mv, slice(None), slice(planes + RADIUS, None))])
    combine(0, 0)
    combine(0, 1)
    template_pass(0)
    combine(0, 2)
    template_pass(1)
    combine(0, 3)
    load_d.wait()
    template_in(0)
    adjoint(0)
    adj_mate(0)
    combine(1, 0)
    adj_slab(0)
    combine(1, 1)
    combine(1, 2)
    adj_across(0)
    combine(1, 3)
    template_in(1)
    adjoint(1)
    adj_mate(1)
    refresh(0)
    adj_slab(1)
    refresh_pass(0)
    adj_across(1)
    refresh_in(0)
    save_template(0)
    save_template(1)
    gradients(0)
    force(0)
    moved_out(0)
    refresh(1)
    refresh_pass(1)
    refresh_in(1)
    save_template(2)
    save_template(3)
    for b in range(1, n_rb):
        gradients(b)
        force(b)
        moved_out(b)
    for copy in load_k:
        copy.wait()
    for b in range(n_rb):
        wire["mu", b].recv()
        wire["md", b].recv()
    for i_f in range(nf):
        smooth(i_f)
    for item in pending:
        item.sent()
    for copy in saves:
        copy.wait()


def per_device(template, displacement, coil_images, sensitivities):
    nf, planes, wide, ny = displacement.shape
    coils = coil_images.shape[2]
    n_slab = lax.axis_size("slab")
    n_frame = lax.axis_size("frame")
    n_rb, n_chunk, per = wide // ROWS, wide // CHUNK, planes // GROUPS
    deep = planes + 2 * BOUND
    ty_hi, ty_lo = split_table(gauss_table(ny))
    kx_hi, kx_lo = split_table(np.kron(np.eye(planes), gauss_table(wide)))
    side = planes * wide
    any_ = pl.BlockSpec(memory_space=pl.ANY)
    scratch = [
        pltpu.VMEM((n_rb, deep, ROWS, ny), F32),
        pltpu.VMEM((n_rb, deep, ROWS, ny), F32),
        pltpu.VMEM((nf, planes, wide, ny), F32),
        pltpu.VMEM((n_chunk, GROUPS, nf, 2, coils, per, CHUNK, ny), BF16),
        pltpu.VMEM((n_chunk, GROUPS, 2, coils, per, CHUNK, ny), BF16),
        pltpu.VMEM((nf, planes, wide, ny), F32),
        pltpu.VMEM((planes, wide, ny), F32),
        pltpu.VMEM((n_rb, deep, ROWS, ny), F32),
        pltpu.VMEM((n_chunk, deep, ROWS, ny), F32),
        pltpu.VMEM((n_chunk, BOUND, ROWS, ny), F32),
        pltpu.VMEM((n_chunk, BOUND, ROWS, ny), F32),
        pltpu.VMEM((n_chunk, planes, ROWS, ny), F32),
        pltpu.VMEM((n_chunk, planes, ROWS, ny), F32),
        pltpu.VMEM((nf, planes + 2 * RADIUS, wide, ny), F32),
        pltpu.VMEM((n_rb, planes, ROWS, ny), F32),
        pltpu.VMEM((n_rb, planes, ROWS, ny), F32),
        pltpu.VMEM((side, ny), BF16),
        pltpu.VMEM((side, ny), BF16),
        pltpu.VMEM((nf, planes, wide, ny), F32),
        pltpu.VMEM((ny, ny), BF16),
        pltpu.VMEM((ny, ny), BF16),
        pltpu.VMEM((side, side), BF16),
        pltpu.VMEM((side, side), BF16),
        pltpu.SemaphoreType.DMA((48,)),
        pltpu.SemaphoreType.DMA((40,)),
        pltpu.SemaphoreType.DMA((40,)),
    ]
    return pl.pallas_call(
        functools.partial(kernel, (n_slab, nf * n_frame, coils)),
        out_shape=(
            jax.ShapeDtypeStruct((planes, wide, ny), F32),
            jax.ShapeDtypeStruct((nf, planes, wide, ny), F32),
        ),
        in_specs=[any_] * 8,
        out_specs=(any_, any_),
        scratch_shapes=scratch,
        compiler_params=pltpu.CompilerParams(
            collective_id=0, has_side_effects=True, vmem_limit_bytes=50 * 1024 * 1024
        ),
        cost_estimate=pl.CostEstimate(flops=10**8, bytes_accessed=2 * 10**7, transcendentals=0),
    )(template, displacement, coil_images, sensitivities,
      jnp.asarray(ty_hi), jnp.asarray(ty_lo), jnp.asarray(kx_hi), jnp.asarray(kx_lo))


def solution(mesh):
    placed = (
        P("slab", None, None),
        P("frame", "slab", None, None),
        P("frame", None, None, "slab", None, None),
        P(None, None, "slab", None, None),
    )
    return jax.shard_map(
        per_device,
        mesh=mesh,
        in_specs=placed,
        out_specs=(P("slab", None, None), P("frame", "slab", None, None)),
        check_vma=False,
    )
```

time: 173 us -> 61 us (0.35)
  waiting for transfers between devices: 84.5 us -> 0 us
  Pallas kernels: 0 us -> 52.5 us
  starting transfers between devices: 35.7 us -> 0 us
  other arithmetic: 24.9 us -> 0 us
  between operations: 14.3 us -> 0.65 us
  matrix products: 9.17 us -> 0 us
  local copies, waits for them, and re-layouts: 4.17 us -> 7.1 us
    pallas_call x0 -> x1, Pallas kernels: none -> 52.5 us  [per_device(): pl.pallas_call(functools.partial(kernel, (n_slab, nf * n_frame, coils)),...]
    ppermute x8 -> x0, waiting for transfers between devices: 48.3 us -> none  [the longest x4 25.5 us: extended_2(): lax.ppermute(head, axis, [((i + 1) % count, i) for i in range(ends)])]
    psum x1 -> x0, waiting for transfers between devices: 36.2 us -> none  [per_device(): summed = lax.psum(summed_local, 'frame')]
    ppermute x8 -> x0, starting transfers between devices: 35.6 us -> none  [the longest x4 25.9 us: extended_2(): lax.ppermute(head, axis, [((i + 1) % count, i) for i in range(ends)])]
    dot_general x2 -> x0, other arithmetic: 9.31 us -> none  [the longest x1 7.81 us: per_device(): jnp.einsum('fpczxy,pczxy->fzxy', coil_images, sensitivities, preferred_el...]
    dot_general x2 -> x0, matrix products: 9.17 us -> none  [the longest x1 7.16 us: smooth_field(): jnp.einsum('...xy,yw->...xw', summed, table_y, precision=lax.Precision.HI...]
    unnamed x11 -> x14, local copies, waits for them, and re-layouts: 1.6 us -> 7.1 us
    unnamed x2 -> x0, other arithmetic: 4.54 us -> none
  transfers between devices with their start and end apart: 9 -> 0, of which waited for: 7 -> 0; matrix products, arithmetic and copies ran while one was open for 10% -> 0% of each run, Pallas kernels for 0% -> 0%
where the time goes in v1:
time: 61 us; the launch traced here: 60.2 us
  Pallas kernels  52.5 us (86%)
  local copies, waits for them, and re-layouts  7.1 us (12%)
  between operations  0.65 us (1%)
    pallas_call x1, Pallas kernels, per_device(): pl.pallas_call(functools.partial(kernel, (n_slab, nf * n_frame, coils)),...  52.5 us
    unnamed x14, local copies, waits for them, and re-layouts  7.1 us

profile of v1, /device:TPU:8, one launch (start us, length us, event | category | flops | bytes accessed | tf_op | source)
XLA Modules:
  0.0 60.2 jit_solution(13142206928108786338)
XLA Ops:
  0.6 0.0 copy-start
  0.6 1.0 %copy-done = f32[2,8,32,256]{3,2,1,0:T(8,128)S(1)} copy-done((f32[2,8,32,256]{3,2,1,0:T(8,128)S(1)}, f32[2,8,32,256]{3,2,1,0:T(8,128)}, u32[]{:S(2)}) %copy-start) | copy-done | bytes 524312
  1.7 0.0 copy-start.1
  1.7 0.9 %copy-done.1 = f32[8,32,256]{2,1,0:T(8,128)S(1)} copy-done((f32[8,32,256]{2,1,0:T(8,128)S(1)}, f32[8,32,256]{2,1,0:T(8,128)}, u32[]{:S(2)}) %copy-start.1) | copy-done | bytes 262168
  2.6 0.0 copy-start.2
  2.6 0.9 %copy-done.2 = bf16[256,256]{1,0:T(8,128)(2,1)S(1)} copy-done((bf16[256,256]{1,0:T(8,128)(2,1)S(1)}, bf16[256,256]{1,0:T(8,128)(2,1)}, u32[]{:S(2)}) %copy-start.2) | copy-done | bytes 131096
  3.5 0.0 copy-start.3
  3.5 0.9 %copy-done.3 = bf16[256,256]{1,0:T(8,128)(2,1)S(1)} copy-done((bf16[256,256]{1,0:T(8,128)(2,1)S(1)}, bf16[256,256]{1,0:T(8,128)(2,1)}, u32[]{:S(2)}) %copy-start.3) | copy-done | bytes 131096
  4.4 0.0 copy-start.4
  4.4 0.9 %copy-done.4 = bf16[256,256]{1,0:T(8,128)(2,1)S(1)} copy-done((bf16[256,256]{1,0:T(8,128)(2,1)S(1)}, bf16[256,256]{1,0:T(8,128)(2,1)}, u32[]{:S(2)}) %copy-start.4) | copy-done | bytes 131096
  5.3 0.0 copy-start.5
  5.3 0.9 %copy-done.5 = bf16[256,256]{1,0:T(8,128)(2,1)S(1)} copy-done((bf16[256,256]{1,0:T(8,128)(2,1)S(1)}, bf16[256,256]{1,0:T(8,128)(2,1)}, u32[]{:S(2)}) %copy-start.5) | copy-done | bytes 131096
  6.2 52.5 %shard_map.95 = (f32[8,32,256]{2,1,0:T(8,128)S(1)}, f32[2,8,32,256]{3,2,1,0:T(8,128)S(1)}) custom-call(f32[8,32,256]{2,1,0:T(8,128)S(1)} %copy-done.1, f32[2,8,32,256]{3,2,1,0:T(8,128)S(1)} %copy-done, bf16[2,2,24,8,32,256]{5,4,3,2,1,0:T(8,128)(2,1)} %coil.1, bf16[2,24,8,32,256]{4,3,2,1,0:T(8,128)(2,1)} %sens.1, bf16[256,256]{1,0:T(8,128)(2,1)S(1)} %copy-done.5, ...), custom_call_target="tpu_custom_call" | custom-call | flops 100000000 | bytes 20000000 | tf_op jit(solution)/shard_map/pallas_call | solution.py:460
  58.7 0.7 %copy.12 = f32[8,32,256]{2,1,0:T(8,128)} copy(f32[8,32,256]{2,1,0:T(8,128)S(1)} %get-tuple-element.4) | data formatting | bytes 524288
  59.4 0.8 %copy.13 = f32[2,8,32,256]{3,2,1,0:T(8,128)} copy(f32[2,8,32,256]{3,2,1,0:T(8,128)S(1)} %get-tuple-element.5) | data formatting | bytes 1048576
Async XLA Ops:
  0.6 1.0 %copy-start = (f32[2,8,32,256]{3,2,1,0:T(8,128)S(1)}, f32[2,8,32,256]{3,2,1,0:T(8,128)}, u32[]{:S(2)}) copy-start(f32[2,8,32,256]{3,2,1,0:T(8,128)} %disp.1) | copy-start | bytes 1572868
  1.7 0.9 %copy-start.1 = (f32[8,32,256]{2,1,0:T(8,128)S(1)}, f32[8,32,256]{2,1,0:T(8,128)}, u32[]{:S(2)}) copy-start(f32[8,32,256]{2,1,0:T(8,128)} %tmpl.1) | copy-start | bytes 786436
  2.6 0.9 %copy-start.2 = (bf16[256,256]{1,0:T(8,128)(2,1)S(1)}, bf16[256,256]{1,0:T(8,128)(2,1)}, u32[]{:S(2)}) copy-start(bf16[256,256]{1,0:T(8,128)(2,1)} %constant.11.clone.kx_lo_h) | copy-start | bytes 393220
  3.5 0.9 %copy-start.3 = (bf16[256,256]{1,0:T(8,128)(2,1)S(1)}, bf16[256,256]{1,0:T(8,128)(2,1)}, u32[]{:S(2)}) copy-start(bf16[256,256]{1,0:T(8,128)(2,1)} %constant.10.clone.kx_hi_h) | copy-start | bytes 393220
  4.4 0.9 %copy-start.4 = (bf16[256,256]{1,0:T(8,128)(2,1)S(1)}, bf16[256,256]{1,0:T(8,128)(2,1)}, u32[]{:S(2)}) copy-start(bf16[256,256]{1,0:T(8,128)(2,1)} %constant.9.clone.ty_lo_h) | copy-start | bytes 393220
  5.3 0.9 %copy-start.5 = (bf16[256,256]{1,0:T(8,128)(2,1)S(1)}, bf16[256,256]{1,0:T(8,128)(2,1)}, u32[]{:S(2)}) copy-start(bf16[256,256]{1,0:T(8,128)(2,1)} %constant.8.clone.ty_hi_h) | copy-start | bytes 393220

commit v2 on v1

v2 whole, which is shorter than its diff:
```python
import functools

import jax
import jax.numpy as jnp
import numpy as np
from jax import lax
from jax.experimental import pallas as pl
from jax.experimental.pallas import tpu as pltpu
from jax.sharding import PartitionSpec as P

BOUND = 8
RADIUS = 4
ROWS = 8
LANES = 128
CHUNK = 16
GROUPS = 4
MESH = pl.DeviceIdType.MESH
F32 = jnp.float32
BF16 = jnp.bfloat16


def gauss_weights():
    j = np.arange(-RADIUS, RADIUS + 1, dtype=np.float64)
    spread = RADIUS * 0.5
    w = np.exp(-j * j / (2.0 * spread * spread))
    return w / w.sum()


def gauss_table(length):
    w = gauss_weights()
    table = np.zeros((length, length), np.float64)
    for j in range(-RADIUS, RADIUS + 1):
        table += w[j + RADIUS] * np.eye(length, k=j)
    return table


def split_table(table):
    hi = table.astype(np.float32).astype(BF16)
    lo = (table - hi.astype(np.float64)).astype(np.float32).astype(BF16)
    return hi, lo


def locate(d):
    m3 = d >= 0.0
    r = jnp.where(m3, d, d + 8.0)
    m2 = r >= 4.0
    r = jnp.where(m2, r - 4.0, r)
    m1 = r >= 2.0
    r = jnp.where(m1, r - 2.0, r)
    m0 = r >= 1.0
    t = jnp.where(m0, r - 1.0, r)
    return m3, m2, m1, m0, t


def gather_line(place, plane):
    m3, m2, m1, m0, t = place
    a = [plane(j) for j in range(17)]
    b = [jnp.where(m3, a[j + 8], a[j]) for j in range(9)]
    c = [jnp.where(m2, b[j + 4], b[j]) for j in range(5)]
    e = [jnp.where(m1, c[j + 2], c[j]) for j in range(3)]
    lo = jnp.where(m0, e[1], e[0])
    hi = jnp.where(m0, e[2], e[1])
    return lo + t * (hi - lo)


def scatter_line(place, value):
    m3, m2, m1, m0, t = place
    hi = t * value
    lo = value - hi
    zero = jnp.zeros_like(value)
    e = [jnp.where(m0, zero, lo), jnp.where(m0, lo, hi), jnp.where(m0, hi, zero)]

    def spread(src, mask, step):
        n = len(src)
        out = []
        for j in range(n + step):
            low = src[j] if j < n else zero
            high = src[j - step] if j >= step else zero
            out.append(jnp.where(mask, high, low))
        return out

    return spread(spread(spread(e, m1, 2), m2, 4), m3, 8)


def kernel(cfg, tmpl, disp, coil, sens, ty_hi_h, ty_lo_h, kx_hi_h, kx_lo_h, out_t, out_d,
           tx, rx, dv, cb, sb, comb, ener, adj, radj, ra, mv,
           shi, slo, obuf, ty_hi, ty_lo, kx_hi, kx_lo, lsem, ssem, rsem):
    n_slab, frames_all, coils = cfg
    nf, planes, wide, ny = obuf.shape
    n_rb = wide // ROWS
    n_lh = ny // LANES
    n_chunk = wide // CHUNK
    per = planes // GROUPS
    reach = BOUND + RADIUS
    f = lax.axis_index("frame")
    s = lax.axis_index("slab")
    h = lax.rem(f, 2)
    q = lax.div(f, 2)
    o = 1 - q
    mate = f + 1 - 2 * h
    across = f + 2 - 4 * q
    at_slab = {k: lax.rem(s + k + n_slab, n_slab) for k in (-2, -1, 0, 1, 2)}
    exists = {-2: s > 1, -1: s > 0, 0: None, 1: s < n_slab - 1, 2: s < n_slab - 2}

    counter = [0]

    def local(src, dst):
        copy = pltpu.make_async_copy(src, dst, lsem.at[counter[0]])
        counter[0] += 1
        copy.start()
        return copy

    load_t = [local(tmpl.at[:, pl.ds(ROWS * b, ROWS), pl.ds(LANES * l, LANES)], tx.at[b, l, pl.ds(BOUND, planes)])
              for b in range(n_rb) for l in range(n_lh)]
    load_d = local(disp, dv.at[:, pl.ds(RADIUS, planes)])
    load_c = {}
    for c in range(n_chunk):
        for g in range(GROUPS):
            zs, xs = pl.ds(per * g, per), pl.ds(CHUNK * c, CHUNK)
            load_c[c, g] = (
                local(sens.at[:, :, zs, xs, :], sb.at[c, g]),
                local(coil.at[:, :, :, zs, xs, :], cb.at[c, g]),
            )
    load_k = [local(a, b) for a, b in ((ty_hi_h, ty_hi), (ty_lo_h, ty_lo), (kx_hi_h, kx_hi), (kx_lo_h, kx_lo))]

    def clear(ref, *index):
        ref[index] = jnp.zeros_like(ref[index])

    every = slice(None)

    @pl.when(s == 0)
    def _():
        clear(tx, every, every, slice(0, BOUND))
        clear(rx, every, every, slice(0, reach))
        clear(dv, every, slice(0, RADIUS))
        clear(comb, every, slice(0, RADIUS))

    @pl.when(s == 1)
    def _():
        clear(rx, every, every, slice(0, RADIUS))

    @pl.when(s == n_slab - 2)
    def _():
        clear(rx, every, every, slice(planes + reach + BOUND, None))

    @pl.when(s == n_slab - 1)
    def _():
        clear(tx, every, every, slice(BOUND + planes, None))
        clear(rx, every, every, slice(planes + reach, None))
        clear(dv, every, slice(planes + RADIUS, None))
        clear(comb, every, slice(planes + RADIUS, None))

    barrier = pltpu.get_barrier_semaphore()
    near = ((mate, s), (across, s), (f, at_slab[1]), (f, at_slab[-1]))
    for dev in near:
        pl.semaphore_signal(barrier, inc=1, device_id=dev, device_id_type=MESH)
    pl.semaphore_wait(barrier, len(near))

    rcount = [0]
    pending = []

    def maybe(condition, action):
        if condition is None:
            action()
        else:
            pl.when(condition)(action)

    class Remote:
        def __init__(self, src, dst, frame, step=0):
            n = rcount[0]
            rcount[0] += 1
            self.copy = pltpu.make_async_remote_copy(
                src_ref=src, dst_ref=dst, send_sem=ssem.at[n], recv_sem=rsem.at[n],
                device_id=(frame, at_slab[step]), device_id_type=MESH)
            self.send_if, self.recv_if = exists[step], exists[-step]
            maybe(self.send_if, lambda: self.copy.start())
            pending.append(self)

        def recv(self):
            maybe(self.recv_if, lambda: self.copy.wait_recv())

        def sent(self):
            maybe(self.send_if, lambda: self.copy.wait_send())

    own = pl.ds(BOUND, planes)
    low = pl.ds(0, BOUND)
    high = pl.ds(BOUND + planes, BOUND)
    inner = pl.ds(reach, planes)
    wire = {}

    def arrive(*keys):
        for key in keys:
            for item in wire[key]:
                item.recv()

    def template_out(c):
        rb = 2 * c + h
        wire["t", c] = [Remote(tx.at[rb, :, own], tx.at[rb, :, low], f, 1),
                        Remote(tx.at[rb, :, own], tx.at[rb, :, high], f, -1)]

    def template_pass(c):
        rb = 2 * c + h
        arrive(("t", c))
        wire["tf", c] = [Remote(tx.at[rb, :, part], tx.at[rb, :, part], mate) for part in (low, high)]

    def template_in(c):
        arrive(("tf", c))

    def disp_out():
        wire["d"] = [
            Remote(dv.at[:, pl.ds(planes, RADIUS)], dv.at[:, pl.ds(0, RADIUS)], f, 1),
            Remote(dv.at[:, pl.ds(RADIUS, RADIUS)], dv.at[:, pl.ds(planes + RADIUS, RADIUS)], f, -1)]

    def comb_out(c):
        xs = pl.ds(CHUNK * c, CHUNK)
        wire["c", c] = [
            Remote(comb.at[:, pl.ds(planes, RADIUS), xs], comb.at[:, pl.ds(0, RADIUS), xs], f, 1),
            Remote(comb.at[:, pl.ds(RADIUS, RADIUS), xs], comb.at[:, pl.ds(planes + RADIUS, RADIUS), xs], f, -1)]

    def combine(c, g):
        for copy in load_c[c, g]:
            copy.wait()

        def step(zz, _):
            acc = None
            for p in range(2):
                for k in range(coils):
                    w = sb[c, g, p, k, zz].astype(F32)
                    vals = [cb[c, g, i, p, k, zz].astype(F32) * w for i in range(nf)] + [w * w]
                    acc = vals if acc is None else [x + v for x, v in zip(acc, vals)]
            z = per * g + zz
            xs = pl.ds(CHUNK * c, CHUNK)
            for i in range(nf):
                comb[i, RADIUS + z, xs, :] = acc[i]
            ener[z, xs, :] = acc[nf]
            return 0

        lax.fori_loop(0, per, step, 0)

    def adjoint(c):
        def step(i, _):
            l = lax.rem(i, n_lh)
            rb = 2 * c + lax.div(i, n_lh)
            lanes = pl.ds(pl.multiple_of(l * LANES, LANES), LANES)
            rows = pl.ds(pl.multiple_of(rb * ROWS, ROWS), ROWS)
            sums = [None] * (planes + 2 * BOUND)
            for z in range(planes):
                en = ener[z, rows, lanes]
                for i_f in range(nf):
                    place = locate(dv[i_f, RADIUS + z, rows, lanes])
                    warped = gather_line(place, lambda j: tx[rb, l, z + j])
                    value = comb[i_f, RADIUS + z, rows, lanes] - en * warped
                    for j, term in enumerate(scatter_line(place, value)):
                        sums[z + j] = term if sums[z + j] is None else sums[z + j] + term
            for at, total in enumerate(sums):
                adj[rb, l, at] = total
            return 0

        lax.fori_loop(0, 2 * n_lh, step, 0)

    def adj_mate(c):
        wire["am", c] = [Remote(adj.at[2 * c + 1 - h], radj.at[c], mate)]

    def adj_out(c):
        rb = 2 * c + h
        arrive(("am", c))
        for part in (high, low):
            adj[rb, o, part] = adj[rb, o, part] + radj[c, o, part]
        sends = [Remote(adj.at[rb, o, high], ra.at[c, 0], across, 1),
                 Remote(adj.at[rb, o, low], ra.at[c, 1], across, -1)]
        for part in (high, low):
            adj[rb, q, part] = adj[rb, q, part] + radj[c, q, part]
        sends += [Remote(adj.at[rb, q, high], ra.at[c, 2], f, 1),
                  Remote(adj.at[rb, q, low], ra.at[c, 3], f, -1)]
        adj[rb, o, own] = adj[rb, o, own] + radj[c, o, own]
        sends += [Remote(adj.at[rb, o, own], ra.at[c, 4], across)]
        adj[rb, q, own] = adj[rb, q, own] + radj[c, q, own]
        wire["a", c] = sends

    def refresh(c):
        rb = 2 * c + h
        arrive(("a", c))

        total = adj[rb, q, own] + ra[c, 4]
        for up, sides in ((True, (0, 2)), (False, (1, 3))):
            for k in sides:
                ok = exists[-1] if up else exists[1]
                total = total + jnp.where(ok, ra[c, k], 0.0)
        rx[rb, q, inner] = tx[rb, q, own] + total * (1.0 / frames_all)
        mine = rx.at[rb, q]
        tail, head = mine.at[pl.ds(reach + RADIUS, RADIUS)], mine.at[pl.ds(reach, RADIUS)]
        whole = mine.at[inner]
        sends = []
        for frame in (across, f):
            sends += [Remote(tail, mine.at[pl.ds(0, RADIUS)], frame, 2),
                      Remote(head, mine.at[pl.ds(planes + reach + BOUND, RADIUS)], frame, -2)]
        for frame in (across, f):
            sends += [Remote(whole, mine.at[pl.ds(RADIUS, BOUND)], frame, 1),
                      Remote(whole, mine.at[pl.ds(planes + reach, BOUND)], frame, -1)]
        sends += [Remote(whole, whole, across)]
        wire["r", c] = sends

    def refresh_pass(c):
        rb = 2 * c + h
        arrive(("r", c))
        wire["rf", c] = [Remote(rx.at[rb], rx.at[rb], mate)]

    def refresh_in(c):
        arrive(("rf", c))

    saves = []

    def save_template(b):
        for l in range(n_lh):
            saves.append(local(rx.at[b, l, inner], out_t.at[:, pl.ds(ROWS * b, ROWS), pl.ds(LANES * l, LANES)]))

    deep = planes + 2 * RADIUS
    UNROLL = 4

    def mismatch(c):
        def step(i, _):
            col = lax.div(i, deep // UNROLL)
            base = lax.rem(i, deep // UNROLL) * UNROLL
            l = lax.rem(col, n_lh)
            rb = 2 * c + lax.div(col, n_lh)
            lanes = pl.ds(pl.multiple_of(l * LANES, LANES), LANES)
            rows = pl.ds(pl.multiple_of(rb * ROWS, ROWS), ROWS)
            for k in range(UNROLL):
                p = base + k
                for i_f in range(nf):
                    warped = gather_line(locate(dv[i_f, p, rows, lanes]), lambda j: rx[rb, l, p + j])
                    mv[i_f, p, rows, lanes] = comb[i_f, p, rows, lanes] - warped
            return 0

        lax.fori_loop(0, 2 * n_lh * (deep // UNROLL), step, 0)

    def push(b):
        row = lax.broadcasted_iota(jnp.int32, (ROWS, LANES), 0)
        lane = lax.broadcasted_iota(jnp.int32, (ROWS, LANES), 1)
        first, last = row == 0, row == ROWS - 1
        left, right = lane == 0, lane == LANES - 1
        rows = pl.ds(b * ROWS, ROWS)
        zero = jnp.zeros((ROWS, LANES), F32)

        def step(i, _):
            for k in range(UNROLL):
                p = i * UNROLL + k
                at = p + BOUND
                for l in range(n_lh):
                    lanes = pl.ds(l * LANES, LANES)
                    here = rx[b, l, at]
                    before = pltpu.roll(rx[b - 1, l, at], 1, 0) if b > 0 else zero
                    after = pltpu.roll(rx[b + 1, l, at], ROWS - 1, 0) if b < n_rb - 1 else zero
                    prev_x = jnp.where(first, before, pltpu.roll(here, 1, 0))
                    next_x = jnp.where(last, after, pltpu.roll(here, ROWS - 1, 0))
                    before = pltpu.roll(rx[b, l - 1, at], 1, 1) if l > 0 else zero
                    after = pltpu.roll(rx[b, l + 1, at], LANES - 1, 1) if l < n_lh - 1 else zero
                    prev_y = jnp.where(left, before, pltpu.roll(here, 1, 1))
                    next_y = jnp.where(right, after, pltpu.roll(here, LANES - 1, 1))
                    gx = (next_x - prev_x) * 0.5
                    gy = (next_y - prev_y) * 0.5
                    gz = (rx[b, l, at + 1] - rx[b, l, at - 1]) * 0.5
                    floor = gx * gx + gy * gy + gz * gz + 1.0
                    for i_f in range(nf):
                        miss = mv[i_f, p, rows, lanes]
                        mv[i_f, p, rows, lanes] = dv[i_f, p, rows, lanes] + miss * gz / (floor + miss * miss)
            return 0

        lax.fori_loop(0, deep // UNROLL, step, 0)

    weights = [float(w) for w in gauss_weights()]

    def halves(value):
        hi = value.astype(BF16)
        return hi, (value - hi.astype(F32)).astype(BF16)

    def dot3(a_hi, a_lo, b_hi, b_lo):
        dot = functools.partial(jnp.dot, preferred_element_type=F32)
        return dot(a_hi, b_hi) + (dot(a_lo, b_hi) + dot(a_hi, b_lo))

    def smooth(i_f):
        for z in range(planes):
            total = None
            for j in range(2 * RADIUS + 1):
                term = weights[j] * mv[i_f, z + j]
                total = term if total is None else total + term
            hi, lo = halves(total)
            at = pl.ds(z * wide, wide)
            shi[at, :] = hi
            slo[at, :] = lo
        along_y = dot3(shi[...], slo[...], ty_hi[...], ty_lo[...])
        y_hi, y_lo = halves(along_y)
        done = dot3(kx_hi[...], kx_lo[...], y_hi, y_lo)
        obuf[i_f] = (BOUND * jnp.tanh(done * (1.0 / BOUND))).reshape(planes, wide, ny)
        saves.append(local(obuf.at[i_f], out_d.at[i_f]))

    for copy in load_t:
        copy.wait()
    for c in range(n_chunk):
        template_out(c)
    for g in range(GROUPS):
        combine(0, g)
    load_d.wait()
    disp_out()
    combine(1, 0)
    combine(1, 1)
    template_pass(0)
    combine(1, 2)
    combine(1, 3)
    template_pass(1)
    template_in(0)
    adjoint(0)
    adj_mate(0)
    template_in(1)
    adjoint(1)
    adj_mate(1)
    adj_out(0)
    adj_out(1)
    comb_out(0)
    comb_out(1)
    refresh(0)
    refresh(1)
    for copy in load_k:
        copy.wait()
    refresh_pass(0)
    refresh_pass(1)
    arrive("d", ("c", 0), ("c", 1))
    refresh_in(0)
    mismatch(0)
    push(0)
    save_template(0)
    save_template(1)
    refresh_in(1)
    save_template(2)
    save_template(3)
    mismatch(1)
    for b in range(1, n_rb):
        push(b)

    @pl.when(s == 0)
    def _():
        clear(mv, every, slice(0, RADIUS))

    @pl.when(s == n_slab - 1)
    def _():
        clear(mv, every, slice(planes + RADIUS, None))

    for i_f in range(nf):
        smooth(i_f)
    for item in pending:
        item.sent()
    for copy in saves:
        copy.wait()


def per_device(template, displacement, coil_images, sensitivities):
    nf, planes, wide, ny = displacement.shape
    coils = coil_images.shape[2]
    n_slab = lax.axis_size("slab")
    n_frame = lax.axis_size("frame")
    n_rb, n_lh, n_chunk, per = wide // ROWS, ny // LANES, wide // CHUNK, planes // GROUPS
    ty_hi, ty_lo = split_table(gauss_table(ny))
    kx_hi, kx_lo = split_table(np.kron(np.eye(planes), gauss_table(wide)))
    side = planes * wide
    any_ = pl.BlockSpec(memory_space=pl.ANY)

    def columns(lead, depth):
        return pltpu.VMEM((*lead, depth, ROWS, LANES), F32)

    def field(depth):
        return pltpu.VMEM((nf, depth, wide, ny), F32)

    scratch = [
        columns((n_rb, n_lh), planes + 2 * BOUND),
        columns((n_rb, n_lh), planes + 2 * BOUND + 2 * RADIUS),
        field(planes + 2 * RADIUS),
        pltpu.VMEM((n_chunk, GROUPS, nf, 2, coils, per, CHUNK, ny), BF16),
        pltpu.VMEM((n_chunk, GROUPS, 2, coils, per, CHUNK, ny), BF16),
        field(planes + 2 * RADIUS),
        pltpu.VMEM((planes, wide, ny), F32),
        columns((n_rb, n_lh), planes + 2 * BOUND),
        columns((n_chunk, n_lh), planes + 2 * BOUND),
        columns((n_chunk, 5), planes),
        field(planes + 2 * RADIUS),
        pltpu.VMEM((side, ny), BF16),
        pltpu.VMEM((side, ny), BF16),
        field(planes),
        pltpu.VMEM((ny, ny), BF16),
        pltpu.VMEM((ny, ny), BF16),
        pltpu.VMEM((side, side), BF16),
        pltpu.VMEM((side, side), BF16),
        pltpu.SemaphoreType.DMA((48,)),
        pltpu.SemaphoreType.DMA((56,)),
        pltpu.SemaphoreType.DMA((56,)),
    ]
    return pl.pallas_call(
        functools.partial(kernel, (n_slab, nf * n_frame, coils)),
        out_shape=(
            jax.ShapeDtypeStruct((planes, wide, ny), F32),
            jax.ShapeDtypeStruct((nf, planes, wide, ny), F32),
        ),
        in_specs=[any_] * 8,
        out_specs=(any_, any_),
        scratch_shapes=scratch,
        compiler_params=pltpu.CompilerParams(
            collective_id=0, has_side_effects=True, vmem_limit_bytes=62 * 1024 * 1024
        ),
        cost_estimate=pl.CostEstimate(flops=10**8, bytes_accessed=2 * 10**7, transcendentals=0),
    )(template, displacement, coil_images, sensitivities,
      jnp.asarray(ty_hi), jnp.asarray(ty_lo), jnp.asarray(kx_hi), jnp.asarray(kx_lo))


def solution(mesh):
    placed = (
        P("slab", None, None),
        P("frame", "slab", None, None),
        P("frame", None, None, "slab", None, None),
        P(None, None, "slab", None, None),
    )
    return jax.shard_map(
        per_device,
        mesh=mesh,
        in_specs=placed,
        out_specs=(P("slab", None, None), P("frame", "slab", None, None)),
        check_vma=False,
    )
```

time: 61 us -> 46.3 us (0.76)
  Pallas kernels: 52.5 us -> 41.5 us
  local copies, waits for them, and re-layouts: 7.1 us -> 3.55 us
    pallas_call x1, Pallas kernels: 52.5 us -> 41.5 us  [per_device(): pl.pallas_call(functools.partial(kernel, (n_slab, nf * n_frame, coils)),...]
    unnamed x14 -> x2, local copies, waits for them, and re-layouts: 7.1 us -> 3.55 us
where the time goes in v2:
time: 46.3 us; the launch traced here: 45.7 us
  Pallas kernels  41.5 us (90%)
  local copies, waits for them, and re-layouts  3.55 us (8%)
  between operations  0.64 us (1%)
    pallas_call x1, Pallas kernels, per_device(): pl.pallas_call(functools.partial(kernel, (n_slab, nf * n_frame, coils)),...  41.5 us
    unnamed x2, local copies, waits for them, and re-layouts  3.55 us

profile of v2, /device:TPU:8, one launch (start us, length us, event | category | flops | bytes accessed | tf_op | source)
XLA Modules:
  0.0 45.7 jit_solution(592790685839825402)
XLA Ops:
  0.6 41.5 %shard_map.95 = (f32[8,32,256]{2,1,0:T(8,128)}, f32[2,8,32,256]{3,2,1,0:T(8,128)}) custom-call(f32[8,32,256]{2,1,0:T(8,128)} %tmpl.1, f32[2,8,32,256]{3,2,1,0:T(8,128)} %disp.1, bf16[2,2,24,8,32,256]{5,4,3,2,1,0:T(8,128)(2,1)} %coil.1, bf16[2,24,8,32,256]{4,3,2,1,0:T(8,128)(2,1)} %sens.1, bf16[256,256]{1,0:T(8,128)(2,1)} %constant.8.clone.ty_hi_h, ...), custom_call_target="tpu_custom_call" | custom-call | flops 100000000 | bytes 20000000 | tf_op jit(solution)/shard_map/pallas_call | solution.py:496
  42.1 1.7 %copy.12 = f32[8,32,256]{2,1,0:T(8,128)} copy(f32[8,32,256]{2,1,0:T(8,128)} %get-tuple-element.4) | data formatting | bytes 524288
  43.8 1.9 %copy.13 = f32[2,8,32,256]{3,2,1,0:T(8,128)} copy(f32[2,8,32,256]{3,2,1,0:T(8,128)} %get-tuple-element.5) | data formatting | bytes 1048576

commit v3 on v2

--- a/solution.py
+++ b/solution.py
@@ -288,25 +288,39 @@
                 total = total + jnp.where(ok, ra[c, k], 0.0)
         rx[rb, q, inner] = tx[rb, q, own] + total * (1.0 / frames_all)
         mine = rx.at[rb, q]
-        tail, head = mine.at[pl.ds(reach + RADIUS, RADIUS)], mine.at[pl.ds(reach, RADIUS)]
         whole = mine.at[inner]
         sends = []
-        for frame in (across, f):
-            sends += [Remote(tail, mine.at[pl.ds(0, RADIUS)], frame, 2),
-                      Remote(head, mine.at[pl.ds(planes + reach + BOUND, RADIUS)], frame, -2)]
         for frame in (across, f):
             sends += [Remote(whole, mine.at[pl.ds(RADIUS, BOUND)], frame, 1),
                       Remote(whole, mine.at[pl.ds(planes + reach, BOUND)], frame, -1)]
         sends += [Remote(whole, whole, across)]
         wire["r", c] = sends
 
+    def far_out(c):
+        mine = rx.at[2 * c + h, q]
+        tail, head = mine.at[pl.ds(reach + RADIUS, RADIUS)], mine.at[pl.ds(reach, RADIUS)]
+        wire["far", c] = []
+        for frame in (across, f):
+            wire["far", c] += [Remote(tail, mine.at[pl.ds(0, RADIUS)], frame, 2),
+                               Remote(head, mine.at[pl.ds(planes + reach + BOUND, RADIUS)], frame, -2)]
+
     def refresh_pass(c):
         rb = 2 * c + h
         arrive(("r", c))
-        wire["rf", c] = [Remote(rx.at[rb], rx.at[rb], mate)]
+        near = rx.at[rb, :, pl.ds(RADIUS, planes + 2 * BOUND)]
+        wire["rf", c] = [Remote(near, near, mate)]
 
     def refresh_in(c):
         arrive(("rf", c))
+
+    def far_pass(c):
+        rb = 2 * c + h
+        arrive(("far", c))
+        ends = [rx.at[rb, :, pl.ds(0, RADIUS)], rx.at[rb, :, pl.ds(planes + reach + BOUND, RADIUS)]]
+        wire["ff", c] = [Remote(end, end, mate) for end in ends]
+
+    def far_in(c):
+        arrive(("ff", c))
 
     saves = []
 
@@ -314,27 +328,27 @@
         for l in range(n_lh):
             saves.append(local(rx.at[b, l, inner], out_t.at[:, pl.ds(ROWS * b, ROWS), pl.ds(LANES * l, LANES)]))
 
-    deep = planes + 2 * RADIUS
-    UNROLL = 4
-
-    def mismatch(c):
+    OWN, HALO = (RADIUS, RADIUS), (0, planes + RADIUS)
+
+    def warp(c, group):
+        first, apart = group
+
         def step(i, _):
-            col = lax.div(i, deep // UNROLL)
-            base = lax.rem(i, deep // UNROLL) * UNROLL
+            col = lax.div(i, 2)
+            base = first + apart * lax.rem(i, 2)
             l = lax.rem(col, n_lh)
             rb = 2 * c + lax.div(col, n_lh)
             lanes = pl.ds(pl.multiple_of(l * LANES, LANES), LANES)
             rows = pl.ds(pl.multiple_of(rb * ROWS, ROWS), ROWS)
-            for k in range(UNROLL):
+            for k in range(RADIUS):
                 p = base + k
                 for i_f in range(nf):
-                    warped = gather_line(locate(dv[i_f, p, rows, lanes]), lambda j: rx[rb, l, p + j])
-                    mv[i_f, p, rows, lanes] = comb[i_f, p, rows, lanes] - warped
+                    mv[i_f, p, rows, lanes] = gather_line(locate(dv[i_f, p, rows, lanes]), lambda j: rx[rb, l, p + j])
             return 0
 
-        lax.fori_loop(0, 2 * n_lh * (deep // UNROLL), step, 0)
-
-    def push(b):
+        lax.fori_loop(0, 4 * n_lh, step, 0)
+
+    def push(b, group):
         row = lax.broadcasted_iota(jnp.int32, (ROWS, LANES), 0)
         lane = lax.broadcasted_iota(jnp.int32, (ROWS, LANES), 1)
         first, last = row == 0, row == ROWS - 1
@@ -343,8 +357,8 @@
         zero = jnp.zeros((ROWS, LANES), F32)
 
         def step(i, _):
-            for k in range(UNROLL):
-                p = i * UNROLL + k
+            for k in range(RADIUS):
+                p = group[0] + i * group[1] + k
                 at = p + BOUND
                 for l in range(n_lh):
                     lanes = pl.ds(l * LANES, LANES)
@@ -362,11 +376,11 @@
                     gz = (rx[b, l, at + 1] - rx[b, l, at - 1]) * 0.5
                     floor = gx * gx + gy * gy + gz * gz + 1.0
                     for i_f in range(nf):
-                        miss = mv[i_f, p, rows, lanes]
+                        miss = comb[i_f, p, rows, lanes] - mv[i_f, p, rows, lanes]
                         mv[i_f, p, rows, lanes] = dv[i_f, p, rows, lanes] + miss * gz / (floor + miss * miss)
             return 0
 
-        lax.fori_loop(0, deep // UNROLL, step, 0)
+        lax.fori_loop(0, 2, step, 0)
 
     weights = [float(w) for w in gauss_weights()]
 
@@ -378,13 +392,21 @@
         dot = functools.partial(jnp.dot, preferred_element_type=F32)
         return dot(a_hi, b_hi) + (dot(a_lo, b_hi) + dot(a_hi, b_lo))
 
+    def taps(i_f, z, inside):
+        total = obuf[i_f, z] if not inside else None
+        for j in range(2 * RADIUS + 1):
+            if inside == (RADIUS <= z + j < planes + RADIUS):
+                term = weights[j] * mv[i_f, z + j]
+                total = term if total is None else total + term
+        return total
+
+    def smooth_own(i_f):
+        for z in range(planes):
+            obuf[i_f, z] = taps(i_f, z, True)
+
     def smooth(i_f):
         for z in range(planes):
-            total = None
-            for j in range(2 * RADIUS + 1):
-                term = weights[j] * mv[i_f, z + j]
-                total = term if total is None else total + term
-            hi, lo = halves(total)
+            hi, lo = halves(taps(i_f, z, False))
             at = pl.ds(z * wide, wide)
             shi[at, :] = hi
             slo[at, :] = lo
@@ -408,6 +430,7 @@
     combine(1, 2)
     combine(1, 3)
     template_pass(1)
+    comb_out(0)
     template_in(0)
     adjoint(0)
     adj_mate(0)
@@ -416,26 +439,38 @@
     adj_mate(1)
     adj_out(0)
     adj_out(1)
-    comb_out(0)
-    comb_out(1)
     refresh(0)
     refresh(1)
+    far_out(0)
+    far_out(1)
+    comb_out(1)
     for copy in load_k:
         copy.wait()
     refresh_pass(0)
     refresh_pass(1)
-    arrive("d", ("c", 0), ("c", 1))
     refresh_in(0)
-    mismatch(0)
-    push(0)
+    warp(0, OWN)
+    push(0, OWN)
     save_template(0)
     save_template(1)
     refresh_in(1)
+    warp(1, OWN)
     save_template(2)
     save_template(3)
-    mismatch(1)
+    far_pass(0)
     for b in range(1, n_rb):
-        push(b)
+        push(b, OWN)
+    far_pass(1)
+    for i_f in range(nf):
+        smooth_own(i_f)
+    arrive("d")
+    far_in(0)
+    warp(0, HALO)
+    far_in(1)
+    warp(1, HALO)
+    arrive(("c", 0), ("c", 1))
+    for b in range(n_rb):
+        push(b, HALO)
 
     @pl.when(s == 0)
     def _():
@@ -490,8 +525,8 @@
         pltpu.VMEM((side, side), BF16),
         pltpu.VMEM((side, side), BF16),
         pltpu.SemaphoreType.DMA((48,)),
-        pltpu.SemaphoreType.DMA((56,)),
-        pltpu.SemaphoreType.DMA((56,)),
+        pltpu.SemaphoreType.DMA((64,)),
+        pltpu.SemaphoreType.DMA((64,)),
     ]
     return pl.pallas_call(
         functools.partial(kernel, (n_slab, nf * n_frame, coils)),
@@ -503,11 +538,12 @@
         out_specs=(any_, any_),
         scratch_shapes=scratch,
         compiler_params=pltpu.CompilerParams(
-            collective_id=0, has_side_effects=True, vmem_limit_bytes=62 * 1024 * 1024
+            collective_id=0, has_side_effects=True, vmem_limit_bytes=50 * 1024 * 1024
         ),
         cost_estimate=pl.CostEstimate(flops=10**8, bytes_accessed=2 * 10**7, transcendentals=0),
-    )(template, displacement, coil_images, sensitivities,
-      jnp.asarray(ty_hi), jnp.asarray(ty_lo), jnp.asarray(kx_hi), jnp.asarray(kx_lo))
+    )(*[pltpu.with_memory_space_constraint(x, pltpu.HBM) for x in (
+        template, displacement, coil_images, sensitivities,
+        jnp.asarray(ty_hi), jnp.asarray(ty_lo), jnp.asarray(kx_hi), jnp.asarray(kx_lo))])
 
 
 def solution(mesh):

time: 46.3 us -> 42.7 us (0.922)
  local copies, waits for them, and re-layouts: 3.55 us -> 1.5 us
  Pallas kernels: 41.5 us -> 40.3 us
    unnamed x2, local copies, waits for them, and re-layouts: 3.55 us -> 1.5 us
    pallas_call x1, Pallas kernels: 41.5 us -> 40.3 us  [per_device(): pl.pallas_call(functools.partial(kernel, (n_slab, nf * n_frame, coils)),...]
where the time goes in v3:
time: 42.7 us; the launch traced here: 42.4 us
  Pallas kernels  40.3 us (94%)
  local copies, waits for them, and re-layouts  1.5 us (4%)
  between operations  0.64 us (1%)
    pallas_call x1, Pallas kernels, per_device(): pl.pallas_call(functools.partial(kernel, (n_slab, nf * n_frame, coils)),...  40.3 us
    unnamed x2, local copies, waits for them, and re-layouts  1.5 us

profile of v3, /device:TPU:8, one launch (start us, length us, event | category | flops | bytes accessed | tf_op | source)
XLA Modules:
  0.0 42.4 jit_solution(18364812639997590754)
XLA Ops:
  0.6 40.3 %shard_map.95 = (f32[8,32,256]{2,1,0:T(8,128)S(1)}, f32[2,8,32,256]{3,2,1,0:T(8,128)S(1)}) custom-call(f32[8,32,256]{2,1,0:T(8,128)} %tmpl.1, f32[2,8,32,256]{3,2,1,0:T(8,128)} %disp.1, bf16[2,2,24,8,32,256]{5,4,3,2,1,0:T(8,128)(2,1)} %coil.1, bf16[2,24,8,32,256]{4,3,2,1,0:T(8,128)(2,1)} %sens.1, bf16[256,256]{1,0:T(8,128)(2,1)} %constant.8.clone.ty_hi_h, ...), custom_call_target="tpu_custom_call" | custom-call | flops 100000000 | bytes 20000000 | tf_op jit(solution)/shard_map/pallas_call | solution.py:531
  40.9 0.7 %copy.12 = f32[8,32,256]{2,1,0:T(8,128)} copy(f32[8,32,256]{2,1,0:T(8,128)S(1)} %get-tuple-element.4) | data formatting | bytes 524288
  41.6 0.8 %copy.13 = f32[2,8,32,256]{3,2,1,0:T(8,128)} copy(f32[2,8,32,256]{3,2,1,0:T(8,128)S(1)} %get-tuple-element.5) | data formatting | bytes 1048576

commit v4 on v3

--- a/solution.py
+++ b/solution.py
@@ -84,7 +84,7 @@
 
 def kernel(cfg, tmpl, disp, coil, sens, ty_hi_h, ty_lo_h, kx_hi_h, kx_lo_h, out_t, out_d,
            tx, rx, dv, cb, sb, comb, ener, adj, radj, ra, mv,
-           shi, slo, obuf, ty_hi, ty_lo, kx_hi, kx_lo, lsem, ssem, rsem):
+           slope, bottom, shi, slo, obuf, ty_hi, ty_lo, kx_hi, kx_lo, lsem, ssem, rsem):
     n_slab, frames_all, coils = cfg
     nf, planes, wide, ny = obuf.shape
     n_rb = wide // ROWS
@@ -112,6 +112,37 @@
 
     load_t = [local(tmpl.at[:, pl.ds(ROWS * b, ROWS), pl.ds(LANES * l, LANES)], tx.at[b, l, pl.ds(BOUND, planes)])
               for b in range(n_rb) for l in range(n_lh)]
+    def clear(ref, *index):
+        ref[index] = jnp.zeros_like(ref[index])
+
+    every = slice(None)
+
+    @pl.when(s == 0)
+    def _():
+        clear(tx, every, every, slice(0, BOUND))
+        clear(rx, every, every, slice(0, reach))
+        clear(dv, every, slice(0, RADIUS))
+        clear(comb, every, slice(0, RADIUS))
+
+    @pl.when(s == 1)
+    def _():
+        clear(rx, every, every, slice(0, RADIUS))
+
+    @pl.when(s == n_slab - 2)
+    def _():
+        clear(rx, every, every, slice(planes + reach + BOUND, None))
+
+    @pl.when(s == n_slab - 1)
+    def _():
+        clear(tx, every, every, slice(BOUND + planes, None))
+        clear(rx, every, every, slice(planes + reach, None))
+        clear(dv, every, slice(planes + RADIUS, None))
+        clear(comb, every, slice(planes + RADIUS, None))
+
+    barrier = pltpu.get_barrier_semaphore()
+    near = ((mate, s), (across, s), (f, at_slab[1]), (f, at_slab[-1]))
+    for dev in near:
+        pl.semaphore_signal(barrier, inc=1, device_id=dev, device_id_type=MESH)
     load_d = local(disp, dv.at[:, pl.ds(RADIUS, planes)])
     load_c = {}
     for c in range(n_chunk):
@@ -123,37 +154,6 @@
             )
     load_k = [local(a, b) for a, b in ((ty_hi_h, ty_hi), (ty_lo_h, ty_lo), (kx_hi_h, kx_hi), (kx_lo_h, kx_lo))]
 
-    def clear(ref, *index):
-        ref[index] = jnp.zeros_like(ref[index])
-
-    every = slice(None)
-
-    @pl.when(s == 0)
-    def _():
-        clear(tx, every, every, slice(0, BOUND))
-        clear(rx, every, every, slice(0, reach))
-        clear(dv, every, slice(0, RADIUS))
-        clear(comb, every, slice(0, RADIUS))
-
-    @pl.when(s == 1)
-    def _():
-        clear(rx, every, every, slice(0, RADIUS))
-
-    @pl.when(s == n_slab - 2)
-    def _():
-        clear(rx, every, every, slice(planes + reach + BOUND, None))
-
-    @pl.when(s == n_slab - 1)
-    def _():
-        clear(tx, every, every, slice(BOUND + planes, None))
-        clear(rx, every, every, slice(planes + reach, None))
-        clear(dv, every, slice(planes + RADIUS, None))
-        clear(comb, every, slice(planes + RADIUS, None))
-
-    barrier = pltpu.get_barrier_semaphore()
-    near = ((mate, s), (across, s), (f, at_slab[1]), (f, at_slab[-1]))
-    for dev in near:
-        pl.semaphore_signal(barrier, inc=1, device_id=dev, device_id_type=MESH)
     pl.semaphore_wait(barrier, len(near))
 
     rcount = [0]
@@ -211,11 +211,11 @@
             Remote(dv.at[:, pl.ds(planes, RADIUS)], dv.at[:, pl.ds(0, RADIUS)], f, 1),
             Remote(dv.at[:, pl.ds(RADIUS, RADIUS)], dv.at[:, pl.ds(planes + RADIUS, RADIUS)], f, -1)]
 
-    def comb_out(c):
-        xs = pl.ds(CHUNK * c, CHUNK)
-        wire["c", c] = [
-            Remote(comb.at[:, pl.ds(planes, RADIUS), xs], comb.at[:, pl.ds(0, RADIUS), xs], f, 1),
-            Remote(comb.at[:, pl.ds(RADIUS, RADIUS), xs], comb.at[:, pl.ds(planes + RADIUS, RADIUS), xs], f, -1)]
+    def comb_out(i_f):
+        part = comb.at[i_f]
+        wire["c", i_f] = [
+            Remote(part.at[pl.ds(planes, RADIUS)], part.at[pl.ds(0, RADIUS)], f, 1),
+            Remote(part.at[pl.ds(RADIUS, RADIUS)], part.at[pl.ds(planes + RADIUS, RADIUS)], f, -1)]
 
     def combine(c, g):
         for copy in load_c[c, g]:
@@ -375,12 +375,38 @@
                     gy = (next_y - prev_y) * 0.5
                     gz = (rx[b, l, at + 1] - rx[b, l, at - 1]) * 0.5
                     floor = gx * gx + gy * gy + gz * gz + 1.0
+                    if group is HALO:
+                        slope[i, l, k, rows] = gz
+                        bottom[i, l, k, rows] = floor
+                        continue
                     for i_f in range(nf):
                         miss = comb[i_f, p, rows, lanes] - mv[i_f, p, rows, lanes]
                         mv[i_f, p, rows, lanes] = dv[i_f, p, rows, lanes] + miss * gz / (floor + miss * miss)
             return 0
 
         lax.fori_loop(0, 2, step, 0)
+
+    def push_halo(i_f):
+        def step(i, _):
+            side = lax.div(i, n_lh)
+            l = lax.rem(i, n_lh)
+            lanes = pl.ds(pl.multiple_of(l * LANES, LANES), LANES)
+            for k in range(RADIUS):
+                p = side * (planes + RADIUS) + k
+                gz = slope[side, l, k]
+                miss = comb[i_f, p, :, lanes] - mv[i_f, p, :, lanes]
+                mv[i_f, p, :, lanes] = dv[i_f, p, :, lanes] + miss * gz / (bottom[side, l, k] + miss * miss)
+            return 0
+
+        lax.fori_loop(0, 2 * n_lh, step, 0)
+
+        @pl.when(s == 0)
+        def _():
+            clear(mv, i_f, slice(0, RADIUS))
+
+        @pl.when(s == n_slab - 1)
+        def _():
+            clear(mv, i_f, slice(planes + RADIUS, None))
 
     weights = [float(w) for w in gauss_weights()]
 
@@ -430,7 +456,6 @@
     combine(1, 2)
     combine(1, 3)
     template_pass(1)
-    comb_out(0)
     template_in(0)
     adjoint(0)
     adj_mate(0)
@@ -443,6 +468,7 @@
     refresh(1)
     far_out(0)
     far_out(1)
+    comb_out(0)
     comb_out(1)
     for copy in load_k:
         copy.wait()
@@ -468,19 +494,11 @@
     warp(0, HALO)
     far_in(1)
     warp(1, HALO)
-    arrive(("c", 0), ("c", 1))
     for b in range(n_rb):
         push(b, HALO)
-
-    @pl.when(s == 0)
-    def _():
-        clear(mv, every, slice(0, RADIUS))
-
-    @pl.when(s == n_slab - 1)
-    def _():
-        clear(mv, every, slice(planes + RADIUS, None))
-
     for i_f in range(nf):
+        arrive(("c", i_f))
+        push_halo(i_f)
         smooth(i_f)
     for item in pending:
         item.sent()
@@ -517,6 +535,8 @@
         columns((n_chunk, n_lh), planes + 2 * BOUND),
         columns((n_chunk, 5), planes),
         field(planes + 2 * RADIUS),
+        pltpu.VMEM((2, n_lh, RADIUS, wide, LANES), F32),
+        pltpu.VMEM((2, n_lh, RADIUS, wide, LANES), F32),
         pltpu.VMEM((side, ny), BF16),
         pltpu.VMEM((side, ny), BF16),
         field(planes),

time: 42.7 us -> 41 us (0.960)
  Pallas kernels: 40.3 us -> 38.7 us
    pallas_call x1, Pallas kernels: 40.3 us -> 38.7 us  [per_device(): pl.pallas_call(functools.partial(kernel, (n_slab, nf * n_frame, coils)),...]
where the time goes in v4:
time: 41 us; the launch traced here: 40.9 us
  Pallas kernels  38.7 us (94%)
  local copies, waits for them, and re-layouts  1.5 us (4%)
  between operations  0.64 us (2%)
    pallas_call x1, Pallas kernels, per_device(): pl.pallas_call(functools.partial(kernel, (n_slab, nf * n_frame, coils)),...  38.7 us
    unnamed x2, local copies, waits for them, and re-layouts  1.5 us

profile of v4, /device:TPU:8, one launch (start us, length us, event | category | flops | bytes accessed | tf_op | source)
XLA Modules:
  0.0 40.9 jit_solution(10563001446619759228)
XLA Ops:
  0.6 38.7 %shard_map.95 = (f32[8,32,256]{2,1,0:T(8,128)S(1)}, f32[2,8,32,256]{3,2,1,0:T(8,128)S(1)}) custom-call(f32[8,32,256]{2,1,0:T(8,128)} %tmpl.1, f32[2,8,32,256]{3,2,1,0:T(8,128)} %disp.1, bf16[2,2,24,8,32,256]{5,4,3,2,1,0:T(8,128)(2,1)} %coil.1, bf16[2,24,8,32,256]{4,3,2,1,0:T(8,128)(2,1)} %sens.1, bf16[256,256]{1,0:T(8,128)(2,1)} %constant.8.clone.ty_hi_h, ...), custom_call_target="tpu_custom_call" | custom-call | flops 100000000 | bytes 20000000 | tf_op jit(solution)/shard_map/pallas_call | solution.py:551
  39.4 0.7 %copy.12 = f32[8,32,256]{2,1,0:T(8,128)} copy(f32[8,32,256]{2,1,0:T(8,128)S(1)} %get-tuple-element.4) | data formatting | bytes 524288
  40.1 0.8 %copy.13 = f32[2,8,32,256]{3,2,1,0:T(8,128)} copy(f32[2,8,32,256]{3,2,1,0:T(8,128)S(1)} %get-tuple-element.5) | data formatting | bytes 1048576

commit v5 on v4

--- a/solution.py
+++ b/solution.py
@@ -237,10 +237,8 @@
 
         lax.fori_loop(0, per, step, 0)
 
-    def adjoint(c):
-        def step(i, _):
-            l = lax.rem(i, n_lh)
-            rb = 2 * c + lax.div(i, n_lh)
+    def adjoint(rb):
+        def step(l, _):
             lanes = pl.ds(pl.multiple_of(l * LANES, LANES), LANES)
             rows = pl.ds(pl.multiple_of(rb * ROWS, ROWS), ROWS)
             sums = [None] * (planes + 2 * BOUND)
@@ -256,7 +254,7 @@
                 adj[rb, l, at] = total
             return 0
 
-        lax.fori_loop(0, 2 * n_lh, step, 0)
+        lax.fori_loop(0, n_lh, step, 0)
 
     def adj_mate(c):
         wire["am", c] = [Remote(adj.at[2 * c + 1 - h], radj.at[c], mate)]
@@ -456,17 +454,17 @@
     combine(1, 2)
     combine(1, 3)
     template_pass(1)
-    template_in(0)
-    adjoint(0)
-    adj_mate(0)
-    template_in(1)
-    adjoint(1)
-    adj_mate(1)
+    for c in range(n_chunk):
+        adjoint(2 * c + h)
+    for c in range(n_chunk):
+        template_in(c)
+        adjoint(2 * c + 1 - h)
+        adj_mate(c)
     adj_out(0)
     adj_out(1)
     refresh(0)
+    far_out(0)
     refresh(1)
-    far_out(0)
     far_out(1)
     comb_out(0)
     comb_out(1)
@@ -506,6 +504,14 @@
         copy.wait()
 
 
+def hand_out(t_in, d_in, t_out, d_out, sem):
+    copies = [pltpu.make_async_copy(d_in, d_out, sem.at[0]), pltpu.make_async_copy(t_in, t_out, sem.at[1])]
+    for copy in copies:
+        copy.start()
+    for copy in copies:
+        copy.wait()
+
+
 def per_device(template, displacement, coil_images, sensitivities):
     nf, planes, wide, ny = displacement.shape
     coils = coil_images.shape[2]
@@ -548,7 +554,7 @@
         pltpu.SemaphoreType.DMA((64,)),
         pltpu.SemaphoreType.DMA((64,)),
     ]
-    return pl.pallas_call(
+    results = pl.pallas_call(
         functools.partial(kernel, (n_slab, nf * n_frame, coils)),
         out_shape=(
             jax.ShapeDtypeStruct((planes, wide, ny), F32),
@@ -564,6 +570,14 @@
     )(*[pltpu.with_memory_space_constraint(x, pltpu.HBM) for x in (
         template, displacement, coil_images, sensitivities,
         jnp.asarray(ty_hi), jnp.asarray(ty_lo), jnp.asarray(kx_hi), jnp.asarray(kx_lo))])
+    return pl.pallas_call(
+        hand_out,
+        out_shape=tuple(jax.ShapeDtypeStruct(x.shape, F32) for x in results),
+        in_specs=[pl.BlockSpec(memory_space=pltpu.VMEM)] * 2,
+        out_specs=(any_, any_),
+        scratch_shapes=[pltpu.SemaphoreType.DMA((2,))],
+        cost_estimate=pl.CostEstimate(flops=0, bytes_accessed=16 * planes * wide * ny, transcendentals=0),
+    )(*[pltpu.with_memory_space_constraint(x, pltpu.VMEM) for x in results])
 
 
 def solution(mesh):

time: 41 us -> 40.1 us (0.978)
  local copies, waits for them, and re-layouts: 1.5 us -> 0 us
  Pallas kernels: 38.7 us -> 39.4 us
    unnamed x2 -> x0, local copies, waits for them, and re-layouts: 1.5 us -> none
    pallas_call x0 -> x1, Pallas kernels: none -> 0.89 us  [per_device(): pl.pallas_call(hand_out, out_shape=tuple((jax.ShapeDtypeStruct(x.shape, F...]
where the time goes in v5:
time: 40.1 us; the launch traced here: 40 us
  Pallas kernels  39.4 us (98%)
  between operations  0.64 us (2%)
    pallas_call x1, Pallas kernels, per_device(): pl.pallas_call(functools.partial(kernel, (n_slab, nf * n_frame, coils)),...  38.5 us
    pallas_call x1, Pallas kernels, per_device(): pl.pallas_call(hand_out, out_shape=tuple((jax.ShapeDtypeStruct(x.shape, F...  0.89 us

profile of v5, /device:TPU:8, one launch (start us, length us, event | category | flops | bytes accessed | tf_op | source)
XLA Modules:
  0.0 40.0 jit_solution(9951649276653292786)
XLA Ops:
  0.6 38.5 %shard_map.95 = (f32[8,32,256]{2,1,0:T(8,128)S(1)}, f32[2,8,32,256]{3,2,1,0:T(8,128)S(1)}) custom-call(f32[8,32,256]{2,1,0:T(8,128)} %tmpl.1, f32[2,8,32,256]{3,2,1,0:T(8,128)} %disp.1, bf16[2,2,24,8,32,256]{5,4,3,2,1,0:T(8,128)(2,1)} %coil.1, bf16[2,24,8,32,256]{4,3,2,1,0:T(8,128)(2,1)} %sens.1, bf16[256,256]{1,0:T(8,128)(2,1)} %constant.8.clone.ty_hi_h, ...), custom_call_target="tpu_custom_call" | custom-call | flops 100000000 | bytes 20000000 | tf_op jit(solution)/shard_map/pallas_call | solution.py:557
  39.1 0.9 %shard_map.96 = (f32[8,32,256]{2,1,0:T(8,128)}, f32[2,8,32,256]{3,2,1,0:T(8,128)}) custom-call(f32[8,32,256]{2,1,0:T(8,128)S(1)} %get-tuple-element.4.t_in, f32[2,8,32,256]{3,2,1,0:T(8,128)S(1)} %get-tuple-element.5.d_in), custom_call_target="tpu_custom_call" | custom-call | bytes 1048576 | tf_op jit(solution)/shard_map/pallas_call | solution.py:573
